TPU v7x, 128 devices: a whole 4x4x4 slice. The times are simulated.
128 devices in a mesh: section: 2 (over core), dp: 16 (over y, x), tensor: 4 (over z).
Axes of the slice: x: 4, y: 4, z: 4, core: 2. Of those that a mesh axis runs over, the one named last changes fastest.
Arguments:
- section_ends: bfloat16 [2, 2, 8192, 1536], P('section', None, ('dp', 'tensor')), may hold values from -6 to 6
- norm_gain: bfloat16 [2, 1536], P('section', ('dp', 'tensor')), may hold values from 0.5 to 1.5
- proj_inner: bfloat16 [2, 1536, 2, 3072], P('section', 'dp', None, 'tensor'), may hold values from -0.15625 to 0.15625
- proj_step: bfloat16 [2, 1536, 48], P('section', 'dp', 'tensor'), may hold values from -0.15625 to 0.15625
- proj_state: bfloat16 [2, 1536, 256], P('section', ('dp', 'tensor')), may hold values from -0.15625 to 0.15625
- conv_inner: bfloat16 [2, 5, 3072], P('section', None, ('dp', 'tensor')), may hold values from -0.5 to 0.5
- conv_state: bfloat16 [2, 5, 256], P('section', None, ('dp', 'tensor')), may hold values from -0.5 to 0.5
- gate_gain: bfloat16 [2, 3072], P('section', ('dp', 'tensor')), may hold values from 0.5 to 1.5
- head_params: bfloat16 [2, 3, 48], P('section', None, 'tensor'), may hold values from -5 to 1.5, as said below
- proj_output: bfloat16 [2, 3072, 1536], P('section', 'tensor', 'dp'), may hold values from -0.109375 to 0.109375
Outputs:
- section_results: float32 [2, 2, 8192, 1536], P('section', None, ('dp', 'tensor'))
- grad_norm_gain: float32 [2, 1536], P('section', ('dp', 'tensor'))
- grad_proj_inner: float32 [2, 1536, 2, 3072], P('section', 'dp', None, 'tensor')
- grad_proj_step: float32 [2, 1536, 48], P('section', 'dp', 'tensor')
- grad_proj_state: float32 [2, 1536, 256], P('section', ('dp', 'tensor'))
- grad_conv_inner: float32 [2, 5, 3072], P('section', None, ('dp', 'tensor'))
- grad_conv_state: float32 [2, 5, 256], P('section', None, ('dp', 'tensor'))
- grad_gate_gain: float32 [2, 3072], P('section', ('dp', 'tensor'))
- grad_head_params: float32 [2, 3, 48], P('section', None, 'tensor')
- grad_proj_output: float32 [2, 3072, 1536], P('section', 'tensor', 'dp')
Inputs may be any that keep to these rules, and one draw needn't show every extreme that they name: `head_params`: row 0 lies in -5 to -1, row 1 in -1 to 1.5, row 2 in 0.5 to 1.5.
All inputs are finite; a program needn't handle non-finite values.
Results may differ from a plain program's by a relative error of at most 0.018.
Values may be sent and summed in bfloat16 or wider, within the bound.
No kernel may reach another device: no remote copies, remote signals or barrier semaphores. Data moves between devices by JAX's collectives and lax.ppermute only.
A program may use at most 192 MiB of HBM per device.

v0:
```python
import functools
import math

import jax
import jax.numpy as jnp
from jax import lax
from jax.sharding import Mesh
from jax.sharding import PartitionSpec as P

D = 1536
GROUP = 256
DP = ("dp_0", "dp_1")
DP_TENSOR = ("dp_0", "dp_1", "tensor")


EPS = 1e-05
HIGH = lax.Precision.HIGHEST


def turned_gather(arrays, axis, dims):
    turned = [jnp.moveaxis(a, dim, 0) for a, dim in zip(arrays, dims)]
    both = jnp.concatenate([t.reshape(len(t), -1) for t in turned], axis=1)
    filled, at, done = (lax.all_gather(both, axis, axis=0, tiled=True), 0, [])
    for t, dim in zip(turned, dims):
        share = filled[:, at : at + t[0].size].reshape(-1, *t.shape[1:])
        done.append(jnp.moveaxis(share, 0, dim))
        at += t[0].size
    return tuple(done)


def in_one_piece(arrays, axis, dim, along):
    widths = [math.prod(a.shape[along:]) for a in arrays]
    both = jnp.concatenate(
        [a.reshape(*a.shape[:along], w) for a, w in zip(arrays, widths)], axis=along
    )
    filled = lax.all_gather(both, axis, axis=dim, tiled=True)
    parts = jnp.split(filled, [sum(widths[:k]) for k in range(1, len(widths))], axis=along)
    return tuple(
        (b.reshape(*filled.shape[:along], *a.shape[along:]) for a, b in zip(arrays, parts))
    )


def laid_out(parts, dim):
    parts = jnp.moveaxis(parts, 0, dim)
    lengths = parts.shape
    return parts.reshape(*lengths[:dim], lengths[dim] * lengths[dim + 1], *lengths[dim + 2 :])


def copy_for_each(x, axis):
    copies = jnp.broadcast_to(x, (lax.axis_size(axis), *x.shape))
    return lax.all_to_all(copies, axis, split_axis=0, concat_axis=0, tiled=True)


def collect(x, axis, dim):
    return laid_out(copy_for_each(x, axis), dim)


def over_copies(x, axis):
    return copy_for_each(x, axis).sum(axis=0)


def split_up(x, dim, size):
    lengths = x.shape
    parts = x.reshape(*lengths[:dim], size, lengths[dim] // size, *lengths[dim + 1 :])
    return jnp.moveaxis(parts, dim, 0)


def summed_on_arrival(x, axis, dim):
    size = lax.axis_size(axis)
    parts = lax.all_to_all(split_up(x, dim, size), axis, 0, 0, tiled=True)
    return jnp.sum(parts, axis=0)


def sent_together(arrays, axis, dim, along):
    widths = [a.shape[along] for a in arrays]
    both = jnp.concatenate(arrays, axis=along)
    filled = lax.psum_scatter(both, axis, scatter_dimension=dim, tiled=True)
    return tuple(jnp.split(filled, [sum(widths[:k]) for k in range(1, len(widths))], axis=along))


def passed_along(x, axis, by):
    size = lax.axis_size(axis)
    pairs = [(i, i + by) for i in range(size) if 0 <= i + by < size]
    return lax.ppermute(x, axis, pairs)


def sent_together_2(arrays, axis, dim, along):
    columns = [a.reshape(*a.shape[:along], -1) for a in arrays]
    both = jnp.concatenate(columns, axis=along)
    filled, at, done = (lax.psum_scatter(both, axis, scatter_dimension=dim, tiled=True), 0, [])
    for a, column in zip(arrays, columns):
        share = filled[..., at : at + column.shape[along]]
        done.append(share.reshape(*share.shape[:along], *a.shape[along:]))
        at += column.shape[along]
    return tuple(done)


def over_axes(x, axes):
    return functools.reduce(lax.psum, axes, x)


def plain_dot(left, right):
    return jnp.dot(left, right, preferred_element_type=jnp.float32)


def dot_first(left, right):
    return lax.dot_general(
        left, right, (((0,), (0,)), ((), ())), preferred_element_type=jnp.float32
    )


def dot_last(left, right):
    return lax.dot_general(
        left, right, (((1,), (1,)), ((), ())), preferred_element_type=jnp.float32
    )


def norm_rows(values, gain):
    return values * lax.rsqrt(jnp.mean(values * values, axis=-1, keepdims=True) + EPS) * gain


def rms_back(values, gain, incoming):
    width = values.shape[1]
    factor = lax.rsqrt(jnp.mean(values * values, axis=-1, keepdims=True) + EPS)
    weighted = incoming * gain
    grad_gain = jnp.sum(incoming * values * factor, axis=0)
    grad_values = factor * weighted - values * (factor * factor * factor) / width * jnp.sum(
        weighted * values, axis=-1, keepdims=True
    )
    return (grad_values, grad_gain)


def causal_conv(values, taps):
    width = taps.shape[0] - 1
    length = values.shape[0]
    padded = jnp.pad(values, ((width - 1, 0), (0, 0)))
    total = jnp.zeros_like(values) + taps[width]
    for k in range(width):
        total = total + taps[k] * padded[k : k + length]
    return total


def mixer_core(
    gate_in, inner_in, state_in, step_in, taps_inner, taps_state, step_bias, decay_log, skip_gain
):
    length, channels = inner_in.shape
    head_count = step_in.shape[1]
    headdim = channels // head_count
    states = state_in.shape[1] // 2
    inner_act = jax.nn.silu(causal_conv(inner_in, taps_inner))
    state_act = jax.nn.silu(causal_conv(state_in, taps_state))
    step_size = jax.nn.softplus(step_in + step_bias)
    log_decay = -step_size * jnp.exp(decay_log)
    block_count = length // GROUP
    weighted = (inner_act.reshape(length, head_count, headdim) * step_size[:, :, None]).reshape(
        block_count, GROUP, head_count, headdim
    )
    keys_input = state_act[:, :states].reshape(block_count, GROUP, states)
    queries_read = state_act[:, states:].reshape(block_count, GROUP, states)
    summed = jnp.cumsum(log_decay.reshape(block_count, GROUP, head_count), axis=1)
    summed_heads = jnp.transpose(summed, (0, 2, 1))
    causal = jnp.arange(GROUP)[:, None] >= jnp.arange(GROUP)[None, :]
    gaps_inside = summed_heads[:, :, :, None] - summed_heads[:, :, None, :]
    decays = jnp.where(causal, jnp.exp(jnp.where(causal, gaps_inside, 0.0)), 0.0)
    intersection = jnp.einsum("cin,cjn->cij", queries_read, keys_input, precision=HIGH)
    mixing = decays * intersection[:, None]
    within = jnp.einsum("chij,cjhp->cihp", mixing, weighted, precision=HIGH)
    to_end = jnp.exp(summed[:, -1:, :] - summed)
    block_states = jnp.einsum("cjh,cjn,cjhp->chpn", to_end, keys_input, weighted, precision=HIGH)
    carried = jnp.zeros((head_count, headdim, states), jnp.float32)
    start_list = []
    for block_index in range(block_count):
        start_list.append(carried)
        carried = (
            jnp.exp(summed[block_index, -1])[:, None, None] * carried + block_states[block_index]
        )
    start_states = jnp.stack(start_list)
    across = jnp.einsum(
        "cin,chpn,cih->cihp", queries_read, start_states, jnp.exp(summed), precision=HIGH
    )
    output = (within + across).reshape(length, channels) + inner_act * jnp.repeat(
        skip_gain, headdim
    )
    return output * jax.nn.silu(gate_in)


def shards(
    section_ends,
    norm_gain,
    proj_inner,
    proj_step,
    proj_state,
    conv_inner,
    conv_state,
    gate_gain,
    head_params,
    proj_output,
):
    first_section = lax.axis_index("section") == 0
    tensor_pos = lax.axis_index("tensor")
    tensor_size = lax.axis_size("tensor")
    micro_count = section_ends.shape[1]
    model_width = D
    local_inner = proj_inner.shape[3]
    full_inner = local_inner * tensor_size
    inner_start = tensor_pos * local_inner
    section_data = section_ends[0].astype(jnp.float32)
    dense = turned_gather((proj_inner[0], proj_step[0], proj_output[0]), DP, (0, 0, 1))
    shared = (
        *in_one_piece((norm_gain[0], proj_state[0]), DP_TENSOR, 0, 1),
        lax.all_gather(conv_inner[0], DP_TENSOR, axis=1, tiled=True),
        lax.all_gather(conv_state[0], DP_TENSOR, axis=1, tiled=True),
        lax.all_gather(gate_gain[0], DP_TENSOR, axis=0, tiled=True),
    )
    norm_weight = shared[0].astype(jnp.float32)
    state_weight = shared[1]
    taps_inner = lax.dynamic_slice_in_dim(
        shared[2].astype(jnp.float32), inner_start, local_inner, 1
    )
    taps_state = shared[3].astype(jnp.float32)
    gate_weight = lax.dynamic_slice_in_dim(
        shared[4].astype(jnp.float32), inner_start, local_inner, 0
    )
    head_local = head_params[0].astype(jnp.float32)

    def forward_layer(resid, weights):
        inner_weight, step_weight, output_weight = weights
        normed_own = norm_rows(resid, norm_weight).astype(jnp.bfloat16)
        normed = collect(normed_own, "tensor", 0)
        inner_cols = plain_dot(normed, inner_weight.reshape(model_width, 2 * local_inner))
        step_raw = plain_dot(normed, step_weight)
        state_raw = plain_dot(normed, state_weight)
        gated = mixer_core(
            inner_cols[:, :local_inner],
            inner_cols[:, local_inner:],
            state_raw,
            step_raw,
            taps_inner,
            taps_state,
            head_local[0],
            head_local[1],
            head_local[2],
        )
        square_sum = over_copies(jnp.sum(gated * gated, axis=1), "tensor")
        factor = lax.rsqrt(square_sum / full_inner + EPS)[:, None]
        scaled = (gated * factor * gate_weight).astype(jnp.bfloat16)
        mixed = summed_on_arrival(plain_dot(scaled, output_weight), "tensor", 0)
        kept = (resid, normed_own, normed, inner_cols, step_raw, state_raw, gated, factor, scaled)
        return (resid + mixed, kept)

    def backward_layer(grad_out, kept, weights):
        resid, normed_own, normed, inner_cols, step_raw, state_raw, gated, factor, scaled = kept
        inner_weight, step_weight, output_weight = weights
        grad_rows = collect(grad_out.astype(jnp.bfloat16), "tensor", 0)
        grad_output_w = dot_first(scaled, grad_rows)
        grad_scaled = dot_last(grad_rows, output_weight)
        weighted = grad_scaled * gate_weight
        grad_gate_local = jnp.sum(grad_scaled * gated * factor, axis=0)
        cross = over_copies(jnp.sum(weighted * gated, axis=1), "tensor")[:, None]
        grad_gated = factor * weighted - gated * (factor * factor * factor) / full_inner * cross
        _, pullback = jax.vjp(
            mixer_core,
            inner_cols[:, :local_inner],
            inner_cols[:, local_inner:],
            state_raw,
            step_raw,
            taps_inner,
            taps_state,
            head_local[0],
            head_local[1],
            head_local[2],
        )
        pieces = pullback(grad_gated)
        grad_inner = jnp.concatenate([pieces[0], pieces[1]], axis=1).astype(jnp.bfloat16)
        grad_step = pieces[3].astype(jnp.bfloat16)
        flat_inner = inner_weight.reshape(model_width, 2 * local_inner)
        grad_inner_w = dot_first(normed, grad_inner).reshape(model_width, 2, local_inner)
        grad_step_w = dot_first(normed, grad_step)
        partial_rows = dot_last(grad_inner, flat_inner) + dot_last(grad_step, step_weight)
        grad_normed, grad_state_own = tuple(
            (
                part.astype(jnp.float32)
                for part in sent_together(
                    (partial_rows.astype(jnp.bfloat16), pieces[2].astype(jnp.bfloat16)),
                    "tensor",
                    0,
                    1,
                )
            )
        )
        state_low = grad_state_own.astype(jnp.bfloat16)
        grad_normed = grad_normed + dot_last(state_low, state_weight)
        grad_state_w = dot_first(normed_own, state_low)
        grad_resid, grad_norm_w = rms_back(resid, norm_weight, grad_normed)
        taps_full = lax.dynamic_update_slice_in_dim(
            jnp.zeros((pieces[4].shape[0], full_inner), jnp.float32), pieces[4], inner_start, 1
        )
        gate_full = lax.dynamic_update_slice_in_dim(
            jnp.zeros((full_inner,), jnp.float32), grad_gate_local, inner_start, 0
        )
        head_grad = jnp.stack([pieces[6], pieces[7], pieces[8]])
        grads = (
            grad_inner_w,
            grad_step_w,
            grad_output_w,
            grad_norm_w,
            grad_state_w,
            taps_full,
            pieces[5],
            gate_full,
            head_grad,
        )
        return (grad_out + grad_resid, grads)

    zero_rows = jnp.zeros_like(section_data[0])
    carry_state = {"forward_in": zero_rows, "backward_in": zero_rows, "totals": None}
    kept_list = [None] * (micro_count + 1)
    out_list = [None] * (micro_count + 1)
    grad_list = [None] * (micro_count + 1)

    def forward_tick(tick):
        feed = jnp.where(
            first_section, section_data[min(tick, micro_count - 1)], carry_state["forward_in"]
        )
        result_rows, kept = forward_layer(feed, dense)
        kept_list[tick] = kept
        out_list[tick] = result_rows
        if tick < micro_count:
            carry_state["forward_in"] = passed_along(
                result_rows.astype(jnp.bfloat16), "section", 1
            ).astype(jnp.float32)

    def backward_tick(tick):
        earlier = kept_list[max(tick - 1, 0)]
        later = kept_list[min(tick + 1, micro_count)]
        kept = jax.tree.map(lambda a, b: jnp.where(first_section, a, b), earlier, later)
        grad_in = jnp.where(
            first_section, carry_state["backward_in"], section_data[min(tick, micro_count - 1)]
        )
        grad_rows, grads = backward_layer(grad_in, kept, dense)
        usable = jnp.where(first_section, tick >= 1, tick < micro_count)
        grads = jax.tree.map(lambda v: jnp.where(usable, v, 0.0), grads)
        totals = carry_state["totals"]
        carry_state["totals"] = grads if totals is None else jax.tree.map(jnp.add, totals, grads)
        grad_list[tick] = grad_rows
        if tick < micro_count:
            carry_state["backward_in"] = passed_along(
                grad_rows.astype(jnp.bfloat16), "section", -1
            ).astype(jnp.float32)

    for tick in range(micro_count + 1):
        forward_tick(tick)
    for tick in range(micro_count + 1):
        backward_tick(tick)
    totals = carry_state["totals"]
    section_rows = jnp.stack(
        [jnp.where(first_section, grad_list[m + 1], out_list[m + 1]) for m in range(micro_count)]
    )
    grad_inner_w, grad_step_w, grad_output_w = (
        *tuple(
            (
                part.astype(jnp.float32)
                for part in sent_together_2(
                    (totals[0].astype(jnp.bfloat16), totals[1].astype(jnp.bfloat16)), DP, 0, 1
                )
            )
        ),
        lax.psum_scatter(
            totals[2].astype(jnp.bfloat16), DP, scatter_dimension=1, tiled=True
        ).astype(jnp.float32),
    )
    shared_sums = (
        *sent_together_2((totals[3], totals[4]), DP_TENSOR, 0, 1),
        lax.psum_scatter(totals[5], DP_TENSOR, scatter_dimension=1, tiled=True),
        lax.psum_scatter(totals[6], DP_TENSOR, scatter_dimension=1, tiled=True),
        lax.psum_scatter(totals[7], DP_TENSOR, scatter_dimension=0, tiled=True),
    )
    head_sum = over_axes(totals[8], DP)
    return (
        section_rows[None],
        shared_sums[0][None],
        grad_inner_w[None],
        grad_step_w[None],
        shared_sums[1][None],
        shared_sums[2][None],
        shared_sums[3][None],
        shared_sums[4][None],
        head_sum[None],
        grad_output_w[None],
    )


def solution(mesh):
    split = Mesh(
        mesh.devices.reshape(mesh.shape["section"], 4, 4, mesh.shape["tensor"]),
        ("section", "dp_0", "dp_1", "tensor"),
    )
    placed = (
        P("section", None, DP_TENSOR, None),
        P("section", DP_TENSOR),
        P("section", DP, None, "tensor"),
        P("section", DP, "tensor"),
        P("section", DP_TENSOR, None),
        P("section", None, DP_TENSOR),
        P("section", None, DP_TENSOR),
        P("section", DP_TENSOR),
        P("section", None, "tensor"),
        P("section", "tensor", DP),
    )
    return jax.shard_map(
        shards,
        mesh=split,
        in_specs=placed,
        out_specs=(
            P("section", None, DP_TENSOR, None),
            P("section", DP_TENSOR),
            P("section", DP, None, "tensor"),
            P("section", DP, "tensor"),
            P("section", DP_TENSOR, None),
            P("section", None, DP_TENSOR),
            P("section", None, DP_TENSOR),
            P("section", DP_TENSOR),
            P("section", None, "tensor"),
            P("section", "tensor", DP),
        ),
        check_vma=False,
    )
```

profile of v0, /device:TPU:0, one launch (start us, length us, event | category | flops | bytes accessed | tf_op | source)
XLA Modules:
  0.0 2182.0 jit_solution(11527640309586205198)
XLA Ops:
  11.8 186.5 %all_gather.16 = bf16[1536,257]{1,0:T(8,128)(2,1)S(1)} all-gather(bf16[24,257]{1,0:T(8,128)(2,1)S(1)} %pad_maximum_fusion.11), channel_id=1, replica_groups=mesh['section'=2,'dp_0'=4,'dp_1'=4,'tensor'=4] {'dp_0','dp_1','tensor'}, dimensions={0}, use_global_device_ids=true | all-gather | bytes 801840 | tf_op jit(solution)/shard_map/all_gather | solution.py:36
  205.4 172.3 %all-gather.1 = bf16[1,5,256]{1,0,2:T(2,128)(2,1)S(1)} all-gather(bf16[1,5,4]{1,0,2:T(2,128)(2,1)S(1)} %copy.858), channel_id=3, replica_groups=mesh['section'=2,'dp_0'=4,'dp_1'=4,'tensor'=4] {'dp_0','dp_1','tensor'}, dimensions={2}, use_global_device_ids=true | all-gather | bytes 2600 | tf_op jit(solution)/shard_map/all_gather | solution.py:212
  379.5 175.8 %all-reduce.87 = bf16[3072]{0:T(1024)(128)(2,1)S(1)} all-reduce(bf16[3072]{0:T(1024)(128)(2,1)S(1)} %dynamic-update-slice.8), channel_id=4, replica_groups=mesh['section'=2,'dp_0'=4,'dp_1'=4,'tensor'=4] {'dp_0','dp_1','tensor'}, use_global_device_ids=true, to_apply=%add.87 | all-reduce | flops 3072 | bytes 12288
  555.4 178.0 %all-gather = bf16[1,5,3072]{1,0,2:T(2,128)(2,1)S(1)} all-gather(bf16[1,5,48]{1,0,2:T(2,128)(2,1)S(1)} %copy.850), channel_id=2, replica_groups=mesh['section'=2,'dp_0'=4,'dp_1'=4,'tensor'=4] {'dp_0','dp_1','tensor'}, dimensions={2}, use_global_device_ids=true | all-gather | bytes 31200 | tf_op jit(solution)/shard_map/all_gather | solution.py:211
  738.7 12.0 slice_reduce_fusion.4
  815.1 25.4 %all_to_all.81 = f32[4,128,1536]{2,1,0:T(8,128)} all-to-all(f32[4,128,1536]{2,1,0:T(8,128)S(1)} %bitcast.655), channel_id=1, replica_groups=mesh['section'=2,'dp_0'=4,'dp_1'=4,'tensor'=4] {'tensor'}, dimensions={0} | all-to-all | bytes 6291456 | tf_op jit(solution)/shard_map/all_to_all | solution.py:70
  847.5 24.0 %all_to_all.82 = bf16[4,128,1536]{2,1,0:T(8,128)(2,1)S(1)} all-to-all(bf16[4,128,1536]{2,1,0:T(8,128)(2,1)S(1)} %broadcast_in_dim.315), channel_id=1, replica_groups=mesh['section'=2,'dp_0'=4,'dp_1'=4,'tensor'=4] {'tensor'}, dimensions={0} | all-to-all | bytes 3145728 | tf_op jit(solution)/shard_map/all_to_all | solution.py:51
  930.4 7.5 multiply_reduce_fusion.31
  953.5 18.7 all-to-all-done.5
  982.9 38.0 %all_to_all.83 = f32[4,128,1536]{2,1,0:T(8,128)} all-to-all(f32[4,128,1536]{2,1,0:T(8,128)S(1)} %bitcast.656), channel_id=1, replica_groups=mesh['section'=2,'dp_0'=4,'dp_1'=4,'tensor'=4] {'tensor'}, dimensions={0} | all-to-all | bytes 6291456 | tf_op jit(solution)/shard_map/all_to_all | solution.py:70
  1046.6 9.4 all-to-all-done.8
  1059.4 7.5 broadcast_select_fusion.5
  1120.2 11.7 fusion.37
  1149.1 7.2 bitcast_add_fusion.3
  1160.1 7.1 fusion.141
  1177.3 7.3 multiply_reduce_fusion.23
  1258.4 15.1 all-to-all-done.10
  1337.9 11.5 fusion.39
  1366.7 7.2 bitcast_add_fusion.1
  1377.6 7.1 fusion.135
  1394.7 7.3 multiply_reduce_fusion.19
  1417.7 24.0 %reduce-scatter.15.cloned.1.call-done = bf16[128,1792]{1,0:T(8,128)(2,1)} async-done(((bf16[512,1792]{1,0:T(8,128)(2,1)}), bf16[128,1792]{1,0:T(8,128)(2,1)}) %reduce-scatter.15.cloned.1.call-update) | async-done | bytes 458768 | tf_op jit(solution)/shard_map/reduce_scatter | solution.py:77
  1459.8 16.5 all-to-all-done.12
  1476.3 7.5 multiply_reduce_fusion.9
  1539.9 11.8 fusion.41
  1568.9 7.3 bitcast_add_fusion
  1583.0 7.1 fusion.129
  1693.2 7.4 copy.1048
  1715.6 10.5 psum.14
  1726.1 10.4 psum.15
  1737.2 349.5 %all-reduce.91 = (f32[5,256]{1,0:T(8,128)S(1)}, f32[3072]{0:T(1024)S(1)}) all-reduce(f32[5,256]{1,0:T(8,128)S(1)} %select_add_fusion.3, f32[3072]{0:T(1024)S(1)} %add_dynamic-update-slice_fusion.2), channel_id=11, replica_groups=mesh['section'=2,'dp_0'=4,'dp_1'=4,'tensor'=4] {'dp_0','dp_1','tensor'}, use_global_device_ids=true, to_apply=%region_99.101.clone | all-reduce | flops 4352 | bytes 34816
  2100.3 71.8 %reduce-scatter.21.cloned.1.call-done = bf16[96,1548]{1,0:T(8,128)(2,1)} async-done(((bf16[1536,1548]{1,0:T(8,128)(2,1)}), bf16[96,1548]{1,0:T(8,128)(2,1)}) %reduce-scatter.21.cloned.1.call-update) | async-done | bytes 297232 | tf_op jit(solution)/shard_map/reduce_scatter | solution.py:90
  (1179 shorter events, 700.5 us)
Async XLA Ops:
  7.2 749.3 %all-gather.5.cloned.1.call-start = ((), (), s32[]{:S(2)}) async-start(), calls=%async_computation.21 | async-start | bytes 7938048 | tf_op jit(solution)/shard_map/all_gather | solution.py:23
  198.5 648.7 %copy-start.139 = (f32[1536]{0:T(1024)}, f32[1536]{0:T(1024)S(1)}, u32[]{:S(2)}) copy-start(f32[1536]{0:T(1024)S(1)} %convert_reduce_fusion) | copy-start | bytes 18436
  201.5 176.5 %copy-start.316 = (u32[128]{0:T(128)S(1)}, u32[128]{0:T(128)}, u32[]{:S(2)}) copy-start(u32[128]{0:T(128)} %constant.298) | copy-start | bytes 1540
  201.5 177.8 %copy-start.329 = (bf16[1,48]{1,0:T(2,128)(2,1)S(1)}, bf16[1,48]{1,0:T(2,128)(2,1)}, u32[]{:S(2)}) copy-start(bf16[1,48]{1,0:T(2,128)(2,1)} %param.18) | copy-start | bytes 292
  201.5 549.2 %all-to-all-start = ((bf16[4,128,1536]{2,1,0:T(8,128)(2,1)}), bf16[4,128,1536]{2,1,0:T(8,128)(2,1)S(1)}, u32[]{:S(2)}, u32[]{:S(2)}) async-start(bf16[4,128,1536]{2,1,0:T(8,128)(2,1)} %broadcast_in_dim.310), calls=%async_computation | async-start | bytes 3145728 | tf_op jit(solution)/shard_map/all_to_all | solution.py:51
  205.2 172.6 %copy-start.283 = (f32[1,3,12]{2,1,0:T(4,128)}, f32[1,3,12]{2,1,0:T(4,128)S(1)}, u32[]{:S(2)}) copy-start(f32[1,3,12]{2,1,0:T(4,128)S(1)} %convert_element_type.162) | copy-start | bytes 436
  377.8 378.7 %copy-start.237 = (f32[12]{0:T(128)}, f32[12]{0:T(128)S(1)}, u32[]{:S(2)}) copy-start(f32[12]{0:T(128)S(1)} %get-tuple-element.345) | copy-start | bytes 148
  377.9 378.7 %copy-start.242 = (f32[12]{0:T(128)}, f32[12]{0:T(128)S(1)}, u32[]{:S(2)}) copy-start(f32[12]{0:T(128)S(1)} %get-tuple-element.346) | copy-start | bytes 148
  378.0 417.7 %copy-start.174 = (f32[768]{0:T(1024)}, f32[768]{0:T(1024)S(1)}, u32[]{:S(2)}) copy-start(f32[768]{0:T(1024)S(1)} %mul.1720) | copy-start | bytes 9220
  800.9 8.9 all-to-all-start.1
  842.8 2.6 collective-permute-start
  938.5 8.5 all-to-all-start.4
  948.3 23.8 %all-to-all-start.5 = ((bf16[4,128,1536]{2,1,0:T(8,128)(2,1)}), bf16[4,128,1536]{2,1,0:T(8,128)(2,1)}, u32[]{:S(2)}, u32[]{:S(2)}) async-start(bf16[4,128,1536]{2,1,0:T(8,128)(2,1)} %broadcast_in_dim.317), calls=%async_computation.5 | async-start | bytes 3145728 | tf_op jit(solution)/shard_map/all_to_all | solution.py:51
  1024.2 5.2 collective-permute-start.2
  1026.1 8.5 all-to-all-start.6
  1036.0 20.0 all-to-all-start.8
  1039.7 188.0 %reduce-scatter.13.cloned.1.call-start = ((), (), s32[]{:S(2)}) async-start(), calls=%async_computation.22 | async-start | bytes 2293760 | tf_op jit(solution)/shard_map/reduce_scatter | solution.py:77
  1199.2 87.1 %copy-start.132 = (f32[512,12]{0,1:T(8,128)}, f32[512,12]{0,1:T(8,128)S(1)}, u32[]{:S(2)}) copy-start(f32[512,12]{0,1:T(8,128)S(1)} %get-tuple-element.305) | copy-start | bytes 73732
  1232.5 8.7 collective-permute-start.1
  1238.0 8.5 all-to-all-start.9
  1247.8 25.7 %all-to-all-start.10 = ((bf16[4,128,1536]{2,1,0:T(8,128)(2,1)}), bf16[4,128,1536]{2,1,0:T(8,128)(2,1)}, u32[]{:S(2)}, u32[]{:S(2)}) async-start(bf16[4,128,1536]{2,1,0:T(8,128)(2,1)} %broadcast_in_dim.321), calls=%async_computation.11 | async-start | bytes 3145728 | tf_op jit(solution)/shard_map/all_to_all | solution.py:51
  1280.3 12.7 all-to-all-start.11
  1284.1 157.6 %reduce-scatter.15.cloned.1.call-start = ((), (), s32[]{:S(2)}) async-start(), calls=%async_computation.23 | async-start | bytes 2293760 | tf_op jit(solution)/shard_map/reduce_scatter | solution.py:77
  1445.7 3.6 collective-permute-start.3
  1451.4 25.0 %all-to-all-start.12 = ((bf16[4,128,1536]{2,1,0:T(8,128)(2,1)}), bf16[4,128,1536]{2,1,0:T(8,128)(2,1)S(1)}, u32[]{:S(2)}, u32[]{:S(2)}) async-start(bf16[4,128,1536]{2,1,0:T(8,128)(2,1)} %broadcast_in_dim.323), calls=%async_computation.14 | async-start | bytes 3145728 | tf_op jit(solution)/shard_map/all_to_all | solution.py:51
  1484.4 11.9 all-to-all-start.13
  1488.1 187.5 %reduce-scatter.17.cloned.1.call-start = ((), (), s32[]{:S(2)}) async-start(), calls=%async_computation.24 | async-start | bytes 2293760 | tf_op jit(solution)/shard_map/reduce_scatter | solution.py:77
  1620.1 468.1 %reduce-scatter.23.cloned.1.call-start = ((), (), s32[]{:S(2)}) async-start(), calls=%async_computation.27 | async-start | bytes 1597440
  1638.1 457.5 %reduce-scatter.19.cloned.1.call-start = ((), (), s32[]{:S(2)}) async-start(), calls=%async_computation.25 | async-start | bytes 2506752 | tf_op jit(solution)/shard_map/reduce_scatter | solution.py:368
  1643.8 453.4 %all-reduce.94.cloned.1.call-start = ((), (), s32[]{:S(2)}) async-start(), calls=%async_computation.28 | async-start | bytes 3244032
  1683.4 488.7 %reduce-scatter.21.cloned.1.call-start = ((), (), s32[]{:S(2)}) async-start(), calls=%async_computation.26 | async-start | bytes 5431296 | tf_op jit(solution)/shard_map/reduce_scatter | solution.py:90
  1707.0 382.5 %all-to-all-start.14 = ((f32[4,128,1536]{2,1,0:T(8,128)}), f32[4,128,1536]{2,1,0:T(8,128)}, u32[]{:S(2)}, u32[]{:S(2)}) async-start(f32[4,128,1536]{2,1,0:T(8,128)} %bitcast.654), calls=%async_computation.17 | async-start | bytes 6291456 | tf_op jit(solution)/shard_map/all_to_all | solution.py:70
  (330 other events, 2147.6 us)
Sparse Core Ops, SparseCore 0:
  11.1 69.9 all-gather.4
  1201.3 22.1 reduce-scatter.12
  1416.5 25.1 reduce-scatter.14
  1620.2 29.2 reduce-scatter.16
  1653.7 227.9 reduce-scatter.22
  1884.8 72.1 reduce-scatter.18
  1961.9 130.2 all-reduce.93
  2095.9 76.1 reduce-scatter.20
where the time goes:
time: 2190 us; the launch traced here: 2180 us
  blocking collectives  1170 us (53%)
  matrix products  297 us (14%)
  local copies, waits for them, and re-layouts  275 us (13%)
  other arithmetic  189 us (9%)
  waiting for transfers between devices  177 us (8%)
  starting transfers between devices  51.8 us (2%)
    unnamed x2, blocking collectives  525 us
    all_gather x1, blocking collectives, in_one_piece(): filled = lax.all_gather(both, axis, axis=dim, tiled=True)  186 us
    all_gather x1, blocking collectives, shards(): lax.all_gather(conv_inner[0], DP_TENSOR, axis=1, tiled=True)  178 us
    all_gather x1, blocking collectives, shards(): lax.all_gather(conv_state[0], DP_TENSOR, axis=1, tiled=True)  172 us
    dot_general x12, matrix products, mixer_core(): within = jnp.einsum('chij,cjhp->cihp', mixing, weighted, precision=HIGH)  99.4 us
    all_to_all x11, waiting for transfers between devices, copy_for_each(): return lax.all_to_all(copies, axis, split_axis=0, concat_axis=0, tiled=True)  77.9 us
    unnamed x707, local copies, waits for them, and re-layouts  72.3 us
    reduce_scatter x1, waiting for transfers between devices, sent_together_2(): lax.psum_scatter(both, axis, scatter_dimension=dim, tiled=True)  71.8 us
  transfers between devices with their start and end apart: 24, of which 12 were waited for; matrix products, arithmetic and copies ran while one was open for 9% of the time, Pallas kernels for 0%

commit v1 on v0

v1 whole, which is shorter than its diff:
```python
import jax
import jax.numpy as jnp
import numpy as np
from jax import lax
from jax.experimental import pallas as pl
from jax.experimental.pallas import tpu as pltpu
from jax.sharding import Mesh
from jax.sharding import PartitionSpec as P

D = 1536
SEQ = 512
BLOCK = 128
BLOCKS = SEQ // BLOCK
STATES = 128
CHANNELS = 768
HALF = CHANNELS // 2
HEADS = 12
HEAD_DIM = 64
PAIRS = HEADS // 2
DI = 3072
PAD = 8
EPS = 1e-05
NEG = -1e30
DP = ("dp_0", "dp_1")
DP_TENSOR = ("dp_0", "dp_1", "tensor")
SENT = D + 128
BF = jnp.bfloat16
F32 = jnp.float32
HIGH = lax.Precision.HIGHEST
VMEM = pl.BlockSpec(memory_space=pltpu.VMEM)
SMEM = pl.BlockSpec(memory_space=pltpu.SMEM)
LIMIT = pltpu.CompilerParams(vmem_limit_bytes=56 * 1024 * 1024)


def dot_nn(left, right):
    return lax.dot_general(left, right, (((1,), (0,)), ((), ())), preferred_element_type=F32)


def dot_nt(left, right):
    return lax.dot_general(left, right, (((1,), (1,)), ((), ())), preferred_element_type=F32)


def dot_tn(left, right):
    return lax.dot_general(left, right, (((0,), (0,)), ((), ())), preferred_element_type=F32)


def dot_high(left, right):
    return lax.dot_general(
        left, right, (((1,), (0,)), ((), ())), precision=HIGH, preferred_element_type=F32
    )


def sigmoid(v):
    return 1.0 / (1.0 + jnp.exp(-v))


def softplus(v):
    return jnp.maximum(v, 0.0) + jnp.log1p(jnp.exp(-jnp.abs(v)))


def rows_at(index):
    return pl.ds(pl.multiple_of(index * BLOCK, BLOCK), BLOCK)


def iota(shape, dim):
    return lax.broadcasted_iota(jnp.int32, shape, dim)


def two_parts(v):
    upper = v.astype(BF)
    lower = (v - upper.astype(F32)).astype(BF)
    return upper, lower


def lane_tiles(width):
    return [slice(at, at + 128) for at in range(0, width, 128)]


def conv_rows(padded, taps, out):
    for cols in lane_tiles(out.shape[1]):
        for start in range(0, SEQ, BLOCK):
            total = taps[4:5, cols] + taps[0:1, cols] * padded[start + 5 : start + 5 + BLOCK, cols]
            for k in range(1, 4):
                at = start + 5 + k
                total = total + taps[k : k + 1, cols] * padded[at : at + BLOCK, cols]
            out[start : start + BLOCK, cols] = total


def conv_back(padded_grad, padded, taps, grad_taps, store):
    for cols in lane_tiles(padded.shape[1]):
        sums = [jnp.zeros((1, 128), F32)] * 5
        for start in range(0, SEQ, BLOCK):
            own = padded_grad[start : start + BLOCK, cols]
            total = taps[3:4, cols] * own
            sums[4] = sums[4] + jnp.sum(own, axis=0, keepdims=True)
            for k in range(4):
                at = start + 5 + k
                sums[k] = sums[k] + jnp.sum(own * padded[at : at + BLOCK, cols], axis=0, keepdims=True)
                if k < 3:
                    at = start + 3 - k
                    total = total + taps[k : k + 1, cols] * padded_grad[at : at + BLOCK, cols]
            store(start, cols, total.astype(BF))
        for k in range(5):
            grad_taps[k : k + 1, cols] = sums[k]


def step_terms(raw, heads):
    valid = iota((BLOCK, 128), 1) < HEADS
    raised = jnp.where(valid, raw + heads[0:1, :], -30.0)
    step = softplus(raised)
    log_decay = -step * jnp.exp(heads[1:2, :])
    lower = (iota((BLOCK, BLOCK), 0) >= iota((BLOCK, BLOCK), 1)).astype(F32)
    summed = dot_high(lower, log_decay)
    return raised, step, log_decay, summed, jnp.transpose(summed)


def spread(values, head):
    first = iota((BLOCK, 128), 1) < HEAD_DIM
    return jnp.where(first, values[:, head : head + 1], values[:, head + 1 : head + 2])


def side_by_side(v):
    first = iota(v.shape, 1) < HEAD_DIM
    zero = jnp.zeros_like(v)
    return jnp.concatenate([jnp.where(first, v, zero), jnp.where(first, zero, v)], axis=0)


def place_chunks(place, chunks, held):
    for offset, chunk in zip((0, 3, 1, 2), chunks):
        held[rows_at(lax.rem(place + offset, 4)), :] = chunk[...]


def forward_kernel(with_cotangent, *refs):
    where_ref = refs[0]
    chunks = refs[1:5]
    own_w, other_w, taps_ref, taps_state_ref, heads_ref = refs[5:10]
    refs = refs[10:]
    if with_cotangent:
        cot_chunks, refs = refs[:4], refs[4:]
    normed, zx, ss, y_out, starts = refs[:5]
    outs, refs = refs[5:9], refs[9:]
    if with_cotangent:
        cot, dscaled, stats, refs = refs[0], refs[1], refs[2], refs[3:]
    x_pad, state_pad, x_conv, state_conv, hidden, gated_gain = refs
    place, core = where_ref[0], where_ref[1]
    place_chunks(place, chunks, normed)
    zx[core] = dot_nn(normed[...], own_w[:, :CHANNELS])
    zx[1 - core] = dot_nn(normed[...], other_w[:, :CHANNELS])
    ss[...] = dot_nn(normed[...], own_w[:, CHANNELS + HALF :])
    if with_cotangent:
        place_chunks(place, cot_chunks, cot)
        dscaled[core] = dot_nn(cot[...], own_w[:, CHANNELS : CHANNELS + HALF])
        dscaled[1 - core] = dot_nn(cot[...], other_w[:, CHANNELS : CHANNELS + HALF])
    x_pad[:PAD, :] = jnp.zeros((PAD, CHANNELS), F32)
    x_pad[PAD:, :] = zx[1]
    state_pad[:PAD, :] = jnp.zeros((PAD, 2 * STATES), F32)
    state_pad[PAD:, :] = ss[:, : 2 * STATES]
    hidden[...] = jnp.zeros_like(hidden)
    conv_rows(x_pad, taps_ref, x_conv)
    conv_rows(state_pad, taps_state_ref, state_conv)

    def block(b, carry):
        rows = rows_at(b)
        state_u = state_conv[rows, :]
        state = state_u * sigmoid(state_u)
        keys, reads = state[:, :STATES].astype(BF), state[:, STATES:].astype(BF)
        keys_t = jnp.transpose(state[:, :STATES]).astype(BF)
        _, step, _, summed, summed_t = step_terms(ss[rows, 2 * STATES :], heads_ref)
        meets = dot_nt(reads, keys)
        causal = iota((BLOCK, BLOCK), 0) >= iota((BLOCK, BLOCK), 1)
        squares = jnp.zeros((BLOCK, 128), F32)
        crosses = jnp.zeros((BLOCK, 128), F32)
        for p in range(PAIRS):
            cols = slice(p * 128, (p + 1) * 128)
            half, part = p // 3, slice((p % 3) * 128, (p % 3 + 1) * 128)
            u = x_conv[rows, cols]
            x = u * sigmoid(u)
            weighted = x * spread(step, 2 * p)
            summed_wide = spread(summed, 2 * p)
            grown = jnp.exp(summed_wide)
            to_end = jnp.exp(summed_wide[BLOCK - 1 : BLOCK, :] - summed_wide)
            mixes = []
            for h in (2 * p, 2 * p + 1):
                gaps = summed[:, h : h + 1] - summed_t[h : h + 1, :]
                mixes.append((jnp.exp(jnp.where(causal, gaps, NEG)) * meets).astype(BF))
            within = dot_nn(
                jnp.concatenate(mixes, axis=1), side_by_side(weighted).astype(BF)
            )
            held = hidden[:, cols]
            held_low = held.astype(BF)
            starts[b, :, cols] = held_low
            y = within + grown * dot_nn(reads, held_low) + x * taps_ref[6:7, cols]
            hidden[:, cols] = grown[BLOCK - 1 : BLOCK, :] * held + dot_nn(
                keys_t, (to_end * weighted).astype(BF)
            )
            y_out[rows, cols] = y
            z = zx[0, rows, cols]
            gated = y * z * sigmoid(z)
            squares = squares + gated * gated
            gained = gated * taps_ref[5:6, cols]
            gated_gain[half, rows, part] = gained.astype(BF)
            if with_cotangent:
                crosses = crosses + gained * dscaled[half, rows, part]
        square = jnp.sum(squares, axis=1, keepdims=True)
        upper, lower = two_parts(square)
        lane = iota((BLOCK, 128), 1)
        zero = jnp.zeros((BLOCK, 128), F32)
        tail = jnp.where(
            lane == 0, upper.astype(F32), jnp.where(lane == 1, lower.astype(F32), zero)
        ).astype(BF)
        for o, out in enumerate(outs):
            @pl.when(b == lax.rem(place + o, 4))
            def _(out=out):
                out[:, D:] = tail
        if with_cotangent:
            cross = jnp.sum(crosses, axis=1, keepdims=True)
            both = jnp.where(lane == 0, square, jnp.where(lane == 1, cross, zero))
            stats[:, rows] = jnp.transpose(both)[:8, :]
        return carry

    lax.fori_loop(0, BLOCKS, block, 0)
    for o, out in enumerate(outs):
        rows = rows_at(lax.rem(place + o, 4))
        out[:, :D] = (
            dot_nt(gated_gain[core, rows, :], own_w[:, CHANNELS : CHANNELS + HALF])
            + dot_nt(gated_gain[1 - core, rows, :], other_w[:, CHANNELS : CHANNELS + HALF])
        ).astype(BF)


def shape(*dims, dtype=F32):
    return jax.ShapeDtypeStruct(dims, dtype)


def forward_call(where, chunks, own_w, other_w, taps, taps_state, heads, cot_chunks=None):
    out_shape = [
        shape(SEQ, D, dtype=BF),
        shape(2, SEQ, CHANNELS),
        shape(SEQ, 384),
        shape(SEQ, CHANNELS),
        shape(BLOCKS, STATES, CHANNELS, dtype=BF),
    ]
    out_shape += [shape(BLOCK, SENT, dtype=BF)] * 4
    args = [where, *chunks, own_w, other_w, taps, taps_state, heads]
    if cot_chunks is not None:
        args += list(cot_chunks)
        out_shape += [shape(SEQ, D, dtype=BF), shape(2, SEQ, HALF), shape(8, SEQ)]

    def kernel(*refs):
        forward_kernel(cot_chunks is not None, *refs)

    return pl.pallas_call(
        kernel,
        out_shape=out_shape,
        in_specs=[SMEM] + [VMEM] * (len(args) - 1),
        out_specs=[VMEM] * len(out_shape),
        scratch_shapes=[
            pltpu.VMEM((PAD + SEQ, CHANNELS), F32),
            pltpu.VMEM((PAD + SEQ, 2 * STATES), F32),
            pltpu.VMEM((SEQ, CHANNELS), F32),
            pltpu.VMEM((SEQ, 2 * STATES), F32),
            pltpu.VMEM((STATES, CHANNELS), F32),
            pltpu.VMEM((2, SEQ, HALF), BF),
        ],
        compiler_params=LIMIT,
        name="layer_forward",
    )(*args)


def backward_kernel(last, *refs):
    where_ref = refs[0]
    normed, zx, ss, y_in, starts = refs[1:6]
    own_w, other_w, taps_ref, taps_state_ref, heads_ref, gain_ref = refs[6:12]
    refs = refs[12:]
    if last:
        dscaled, refs = refs[0], refs[1:]
        stat_parts, refs = refs[:4], refs[4:]
    else:
        chunks, refs = refs[:4], refs[4:]
    d_own, d_other, dss, scaled_own, scaled_other = refs[:5]
    outs, refs = refs[5:9], refs[9:]
    grad_taps, grad_taps_state, grad_heads, grad_gain = refs[:4]
    refs = refs[4:]
    if not last:
        rows_grad, refs = refs[0], refs[1:]
    x_pad, state_pad, x_conv, state_conv, du_pad, dstate_pad = refs[:6]
    d_hidden, d_inner, scaled, factors = refs[6:10]
    refs = refs[10:]
    if not last:
        dscaled = refs[0]
    place, core = where_ref[0], where_ref[1]
    x_pad[:PAD, :] = jnp.zeros((PAD, CHANNELS), F32)
    x_pad[PAD:, :] = zx[1]
    state_pad[:PAD, :] = jnp.zeros((PAD, 2 * STATES), F32)
    state_pad[PAD:, :] = ss[:, : 2 * STATES]
    du_pad[SEQ:, :] = jnp.zeros((PAD, CHANNELS), F32)
    dstate_pad[SEQ:, :] = jnp.zeros((PAD, 2 * STATES), F32)
    for ref in (d_hidden, grad_taps, grad_taps_state, grad_heads, grad_gain):
        ref[...] = jnp.zeros_like(ref)
    if last:
        total = stat_parts[0][...] + stat_parts[1][...] + stat_parts[2][...] + stat_parts[3][...]
        factor = lax.rsqrt(total[0:1, :] / DI + EPS)
        cubed = factor * factor * factor / DI * total[1:2, :]
        row = iota((128, SEQ), 0)
        both = jnp.where(row == 0, factor, jnp.where(row == 1, cubed, 0.0))
        for b in range(BLOCKS):
            part = slice(b * BLOCK, (b + 1) * BLOCK)
            factors[part, :] = jnp.transpose(both[:, part])
    else:
        for offset, chunk in zip((0, 3, 1, 2), chunks):
            rows = rows_at(lax.rem(place + offset, 4))
            rows_grad[rows, :] = chunk[:, :D]
            tail = chunk[:, D:].astype(F32)
            factor = tail[:, 0:1] + tail[:, 1:2]
            cross = tail[:, 2:3] + tail[:, 3:4]
            lane = iota((BLOCK, 128), 1)
            cubed = factor * factor * factor / DI * cross
            factors[rows, :] = jnp.where(lane == 0, factor, jnp.where(lane == 1, cubed, 0.0))
        dscaled[core] = dot_nn(rows_grad[...], own_w[:, CHANNELS : CHANNELS + HALF])
        dscaled[1 - core] = dot_nn(rows_grad[...], other_w[:, CHANNELS : CHANNELS + HALF])

    conv_rows(x_pad, taps_ref, x_conv)
    conv_rows(state_pad, taps_state_ref, state_conv)

    def block(turn, carry):
        b = BLOCKS - 1 - turn
        rows = rows_at(b)
        state_u = state_conv[rows, :]
        state_s = sigmoid(state_u)
        state = state_u * state_s
        keys, reads = state[:, :STATES].astype(BF), state[:, STATES:].astype(BF)
        reads_t = jnp.transpose(state[:, STATES:]).astype(BF)
        raised, step, log_decay, summed, summed_t = step_terms(ss[rows, 2 * STATES :], heads_ref)
        meets_t = dot_nt(keys, reads)
        causal_t = iota((BLOCK, BLOCK), 1) >= iota((BLOCK, BLOCK), 0)
        fac = factors[rows, :][:, 0:1]
        cub = factors[rows, :][:, 1:2]
        d_meets_t = jnp.zeros((BLOCK, BLOCK), F32)
        d_keys = jnp.zeros((BLOCK, STATES), F32)
        d_reads = jnp.zeros((BLOCK, STATES), F32)
        head_sums = jnp.zeros((2 * BLOCK, 128), F32)
        last_row = iota((BLOCK, 128), 0) == BLOCK - 1
        for p in range(PAIRS):
            cols = slice(p * 128, (p + 1) * 128)
            half, part = p // 3, slice((p % 3) * 128, (p % 3 + 1) * 128)
            u = x_conv[rows, cols]
            us = sigmoid(u)
            x = u * us
            step_wide = spread(step, 2 * p)
            summed_wide = spread(summed, 2 * p)
            grown = jnp.exp(summed_wide)
            end = grown[BLOCK - 1 : BLOCK, :]
            to_end = jnp.exp(summed_wide[BLOCK - 1 : BLOCK, :] - summed_wide)
            skip = taps_ref[6:7, cols]
            gain = taps_ref[5:6, cols]
            z = zx[0, rows, cols]
            zs = sigmoid(z)
            z_act = z * zs
            y = y_in[rows, cols]
            gated = y * z_act
            incoming = dscaled[half, rows, part]
            lifted = gated * fac
            scaled[half, rows, part] = (lifted * gain).astype(BF)
            grad_taps[5:6, cols] += jnp.sum(incoming * lifted, axis=0, keepdims=True)
            d_gated = fac * (gain * incoming) - gated * cub
            dy = d_gated * z_act
            d_inner[0, rows, cols] = (d_gated * y * (zs + z_act * (1.0 - zs))).astype(BF)
            dy_low = dy.astype(BF)
            weighted = x * step_wide
            weighted_low = weighted.astype(BF)
            dy_grown = (dy * grown).astype(BF)
            held_low = starts[b, :, cols]
            dh = d_hidden[:, cols]
            dh_low = dh.astype(BF)
            d_reads = d_reads + dot_nt(dy_grown, held_low)
            kept = dot_nn(keys, dh_low) * to_end
            d_keys = d_keys + dot_nt((to_end * weighted).astype(BF), dh_low)
            decays = []
            for h in (2 * p, 2 * p + 1):
                gaps = summed_t[h : h + 1, :] - summed[:, h : h + 1]
                decays.append(jnp.exp(jnp.where(causal_t, gaps, NEG)))
            mixes = jnp.concatenate([(d * meets_t).astype(BF) for d in decays], axis=1)
            d_weighted = dot_nn(mixes, side_by_side(dy).astype(BF)) + kept
            d_mixes = dot_nt(side_by_side(weighted).astype(BF), dy_low)
            d_meets_t = d_meets_t + d_mixes[:BLOCK] * decays[0] + d_mixes[BLOCK:] * decays[1]
            dx = skip * dy + d_weighted * step_wide
            weighted_f = weighted_low.astype(F32)
            moved = dy_low.astype(F32) * (y - skip * x) - weighted_f * d_weighted
            extra = jnp.sum(weighted_f * kept, axis=0, keepdims=True) + end * jnp.sum(
                dh * held_low.astype(F32), axis=0, keepdims=True
            )
            moved = jnp.where(last_row, moved + extra, moved)
            upper, lower = two_parts(jnp.concatenate([moved, x * d_weighted], axis=0))
            picks = (
                iota((256, 128), 1) == 2 * p + (iota((256, 128), 0) % 128) // HEAD_DIM
            ).astype(BF)
            head_sums = head_sums + dot_nn(jnp.concatenate([upper, lower], axis=1), picks)
            grad_taps[6:7, cols] += jnp.sum(dy * x, axis=0, keepdims=True)
            du_pad[rows, cols] = dx * (us + x * (1.0 - us))
            d_hidden[:, cols] = end * dh + dot_nn(reads_t, dy_grown)
        d_reads = d_reads + dot_nn(jnp.transpose(d_meets_t).astype(BF), keys)
        d_keys = d_keys + dot_nn(d_meets_t.astype(BF), reads)
        d_state = jnp.concatenate([d_keys, d_reads], axis=1)
        d_state = d_state * (state_s + state * (1.0 - state_s))
        dstate_pad[rows, :] = d_state
        upper_tri = (iota((BLOCK, BLOCK), 1) >= iota((BLOCK, BLOCK), 0)).astype(F32)
        d_decay = dot_high(upper_tri, head_sums[:BLOCK])
        d_step = head_sums[BLOCK:] - d_decay * jnp.exp(heads_ref[1:2, :])
        d_raw = d_step * sigmoid(raised)
        dss[rows, 2 * STATES :] = d_raw.astype(BF)
        grad_heads[0:1, :] += jnp.sum(d_raw, axis=0, keepdims=True)
        grad_heads[1:2, :] += jnp.sum(d_decay * log_decay, axis=0, keepdims=True)
        return carry

    lax.fori_loop(0, BLOCKS, block, 0)

    def store_inner(start, cols, value):
        d_inner[1, start : start + BLOCK, cols] = value

    def store_state(start, cols, value):
        dss[start : start + BLOCK, cols] = value

    conv_back(du_pad, x_pad, taps_ref, grad_taps, store_inner)
    conv_back(dstate_pad, state_pad, taps_state_ref, grad_taps_state, store_state)
    picks = (iota((CHANNELS, 128), 1) == iota((CHANNELS, 128), 0) // HEAD_DIM).astype(F32)
    grad_heads[2:3, :] = dot_high(grad_taps[...], picks)[6:7, :]
    for o, out in enumerate(outs):
        rows = rows_at(lax.rem(place + o, 4))
        part = (
            dot_nt(d_inner[core, rows, :], own_w[:, :CHANNELS])
            + dot_nt(d_inner[1 - core, rows, :], other_w[:, :CHANNELS])
            + dot_nt(dss[rows, :], own_w[:, CHANNELS + HALF :])
        )
        grad_gain[...] += jnp.sum(part * normed[rows, :].astype(F32), axis=0, keepdims=True)
        out[...] = part.astype(BF)
    grad_gain[...] = grad_gain[...] / gain_ref[...]
    d_own[...] = d_inner[core]
    d_other[...] = d_inner[1 - core]
    scaled_own[...] = scaled[core]
    scaled_other[...] = scaled[1 - core]


def backward_call(where, kept, own_w, other_w, taps, taps_state, heads, gain, last, extra):
    args = [where, *kept, own_w, other_w, taps, taps_state, heads, gain, *extra]
    out_shape = [
        shape(SEQ, CHANNELS, dtype=BF),
        shape(SEQ, CHANNELS, dtype=BF),
        shape(SEQ, 384, dtype=BF),
        shape(SEQ, HALF, dtype=BF),
        shape(SEQ, HALF, dtype=BF),
    ]
    out_shape += [shape(BLOCK, D, dtype=BF)] * 4
    out_shape += [shape(8, CHANNELS), shape(8, 2 * STATES), shape(8, 128), shape(1, D)]
    scratch = [
        pltpu.VMEM((PAD + SEQ, CHANNELS), F32),
        pltpu.VMEM((PAD + SEQ, 2 * STATES), F32),
        pltpu.VMEM((SEQ, CHANNELS), F32),
        pltpu.VMEM((SEQ, 2 * STATES), F32),
        pltpu.VMEM((PAD + SEQ, CHANNELS), F32),
        pltpu.VMEM((PAD + SEQ, 2 * STATES), F32),
        pltpu.VMEM((STATES, CHANNELS), F32),
        pltpu.VMEM((2, SEQ, CHANNELS), BF),
        pltpu.VMEM((2, SEQ, HALF), BF),
        pltpu.VMEM((SEQ, 128), F32),
    ]
    if not last:
        out_shape += [shape(SEQ, D, dtype=BF)]
        scratch += [pltpu.VMEM((2, SEQ, HALF), F32)]

    def kernel(*refs):
        backward_kernel(last, *refs)

    return pl.pallas_call(
        kernel,
        out_shape=out_shape,
        in_specs=[SMEM] + [VMEM] * (len(args) - 1),
        out_specs=[VMEM] * len(out_shape),
        scratch_shapes=scratch,
        compiler_params=LIMIT,
        name="layer_backward",
    )(*args)


def norm_kernel(rows_ref, gain_ref, out):
    v = rows_ref[...].astype(F32)
    q = lax.rsqrt(jnp.mean(v * v, axis=1, keepdims=True) + EPS)
    out[...] = (v * q * gain_ref[...]).astype(BF)


def norm_call(rows, gain):
    return pl.pallas_call(
        norm_kernel,
        out_shape=shape(BLOCK, D, dtype=BF),
        in_specs=[VMEM] * 2,
        out_specs=VMEM,
        name="norm_rows",
    )(rows, gain)


def arrived(parts):
    return sum((part[...].astype(F32) for part in parts[1:]), parts[0][...].astype(F32))


def after_first_kernel(rows_ref, a, b, c, d, gain_ref, hidden, normed, mixed, factor_out):
    total = arrived((a, b, c, d))
    mixed[...] = total[:, :D]
    square = total[:, D : D + 1] + total[:, D + 1 : D + 2]
    factor = lax.rsqrt(square / DI + EPS)
    factor_out[...] = jnp.broadcast_to(factor, (BLOCK, 128))
    low = (rows_ref[...].astype(F32) + factor * total[:, :D]).astype(BF)
    hidden[...] = low
    v = low.astype(F32)
    q = lax.rsqrt(jnp.mean(v * v, axis=1, keepdims=True) + EPS)
    normed[...] = (v * q * gain_ref[...]).astype(BF)


def after_first_call(rows, parts, gain):
    return pl.pallas_call(
        after_first_kernel,
        out_shape=[
            shape(BLOCK, D, dtype=BF),
            shape(BLOCK, D, dtype=BF),
            shape(BLOCK, D),
            shape(BLOCK, 128),
        ],
        in_specs=[VMEM] * 6,
        out_specs=[VMEM] * 4,
        name="between_layers",
    )(rows, *parts, gain)


def after_last_kernel(rows_ref, a, b, c, d, result):
    total = arrived((a, b, c, d))
    square = total[:, D : D + 1] + total[:, D + 1 : D + 2]
    factor = lax.rsqrt(square / DI + EPS)
    result[...] = rows_ref[...].astype(F32) + factor * total[:, :D]


def after_last_call(rows, parts):
    return pl.pallas_call(
        after_last_kernel,
        out_shape=shape(BLOCK, D),
        in_specs=[VMEM] * 5,
        out_specs=VMEM,
        name="last_rows",
    )(rows, *parts)


def rows_back(rows_ref, parts, gain_ref, grad_ref):
    incoming = arrived(parts)
    v = rows_ref[...].astype(F32)
    q = lax.rsqrt(jnp.mean(v * v, axis=1, keepdims=True) + EPS)
    weighted = incoming * gain_ref[...]
    inner = jnp.sum(weighted * v, axis=1, keepdims=True)
    return grad_ref[...].astype(F32) + q * weighted - v * (q * q * q / D * inner)


def back_last_kernel(rows_ref, a, b, c, d, gain_ref, grad_ref, mixed_ref, factor_ref, out):
    low = rows_back(rows_ref, (a, b, c, d), gain_ref, grad_ref).astype(BF)
    out[:, :D] = low
    cross = jnp.sum(low.astype(F32) * mixed_ref[...], axis=1, keepdims=True)
    factor = factor_ref[:, 0:1]
    pieces = [*two_parts(factor), *two_parts(cross)]
    lane = iota((BLOCK, 128), 1)
    tail = jnp.zeros((BLOCK, 128), F32)
    for k, piece in enumerate(pieces):
        tail = jnp.where(lane == k, piece.astype(F32), tail)
    out[:, D:] = tail.astype(BF)


def back_last_call(rows, parts, gain, grad, mixed, factor):
    return pl.pallas_call(
        back_last_kernel,
        out_shape=shape(BLOCK, SENT, dtype=BF),
        in_specs=[VMEM] * 9,
        out_specs=VMEM,
        name="between_layers_back",
    )(rows, *parts, gain, grad, mixed, factor)


def back_first_kernel(rows_ref, a, b, c, d, gain_ref, grad_ref, out):
    out[...] = rows_back(rows_ref, (a, b, c, d), gain_ref, grad_ref[:, :D])


def back_first_call(rows, parts, gain, grad):
    return pl.pallas_call(
        back_first_kernel,
        out_shape=shape(BLOCK, D),
        in_specs=[VMEM] * 7,
        out_specs=VMEM,
        name="first_rows_back",
    )(rows, *parts, gain, grad)


def swap(v):
    return lax.ppermute(v, "section", [(0, 1), (1, 0)])


def turn(v, by):
    return lax.ppermute(v, "tensor", [(i, (i + by) % 4) for i in range(4)])


def spread_rows(v):
    return (v, turn(v, 1), turn(v, -1), turn(v, 2))


def meet(parts):
    own, ahead, across, behind = parts
    return (own, turn(ahead, 1), turn(behind, -1), turn(across, 2))


def pick(v, index, axis):
    return lax.dynamic_index_in_dim(v, index, axis, keepdims=False)


def shards(
    section_ends,
    norm_gain,
    proj_inner,
    proj_step,
    proj_state,
    conv_inner,
    conv_state,
    gate_gain,
    head_params,
    proj_output,
):
    core = lax.axis_index("section")
    place = lax.axis_index("tensor")
    is_first = core == 0
    where = jnp.stack([place, core]).astype(jnp.int32)

    ends = section_ends[0]
    got_rows = swap(pick(ends, 1 - core, 0))
    rows_in = jnp.where(is_first, ends[0], got_rows)
    cot = jnp.where(is_first, got_rows, ends[1])

    inner = proj_inner[0]
    out_t = proj_output[0].T.reshape(96, 2, HALF)
    packed = jnp.concatenate(
        [
            proj_state[0].reshape(-1),
            norm_gain[0],
            conv_inner[0].reshape(-1),
            gate_gain[0],
            conv_state[0].reshape(-1),
            jnp.zeros((32 * 256 - 6144 - 332,), BF),
        ]
    ).reshape(32, 256)
    filled = lax.all_gather(packed, "tensor", axis=0).reshape(4, 32 * 256)
    state_rows = filled[:, :6144].reshape(96, 256)
    norm_col = filled[:, 6144:6168].reshape(96, 1)
    inner_cols = filled[:, 6168:6408].reshape(4, 5, 48).transpose(0, 2, 1).reshape(192, 5)
    gate_col = filled[:, 6408:6456].reshape(192, 1)
    both = jnp.concatenate([inner_cols, gate_col], axis=1)
    both = both.reshape(2, 96, 6).transpose(1, 0, 2).reshape(96, 12)
    state_cols = filled[:, 6456:6476].reshape(4, 5, 4).transpose(0, 2, 1).reshape(16, 5)
    state_cols = jnp.pad(state_cols, ((0, 80), (0, 0)))
    misc = jnp.concatenate(
        [proj_step[0], both, norm_col, state_cols, jnp.zeros((96, 128 - 30), BF)], axis=1
    )
    rest = jnp.concatenate([state_rows, misc], axis=1)
    keep = jnp.concatenate([pick(inner, core, 1), pick(out_t, core, 1), rest], axis=1)
    give = jnp.concatenate([pick(inner, 1 - core, 1), pick(out_t, 1 - core, 1), rest], axis=1)
    got = swap(give)
    own_w, other_w, taps, taps_state, gains = [], [], [], [], []
    for layer in range(2):
        shard = jnp.where(core == layer, keep, got)
        full = lax.all_gather(shard, DP, axis=0, tiled=True)
        own_w.append(full)
        other_w.append(swap(full[:, : CHANNELS + HALF]))
        small = full[:, CHANNELS + HALF + 256 :].astype(F32)
        gains.append(small[:, 24].reshape(1, D))
        mine = lax.dynamic_slice_in_dim(small, place * 384, 384, 0)[:, 12:24]
        taps.append(mine.reshape(4, 96, 2, 6).transpose(3, 0, 2, 1).reshape(6, CHANNELS))
        taps_state.append(
            jnp.pad(
                small.reshape(16, 96, 128)[:, :16, 25:30].reshape(256, 5).T, ((0, 3), (0, 0))
            )
        )
    heads_own = head_params[0].astype(F32)
    heads_got = swap(head_params[0]).astype(F32)
    heads = []
    for layer in range(2):
        h = jnp.where(core == layer, heads_own, heads_got)
        taps[layer] = jnp.concatenate(
            [taps[layer], jnp.repeat(h[2], HEAD_DIM)[None], jnp.zeros((1, CHANNELS), F32)], axis=0
        )
        heads.append(jnp.pad(h, ((0, 5), (0, 128 - HEADS))))

    normed_0 = norm_call(rows_in, gains[0])
    kept_0 = forward_call(
        where, spread_rows(normed_0), own_w[0], other_w[0], taps[0], taps_state[0], heads[0]
    )
    hidden, normed_1, mixed_0, factor_0 = after_first_call(rows_in, meet(kept_0[5:9]), gains[1])
    kept_1 = forward_call(
        where,
        spread_rows(normed_1),
        own_w[1],
        other_w[1],
        taps[1],
        taps_state[1],
        heads[1],
        spread_rows(cot),
    )
    cot_rows, dscaled_1, stats = kept_1[9:]
    back_1 = backward_call(
        where,
        kept_1[:5],
        own_w[1],
        other_w[1],
        taps[1],
        taps_state[1],
        heads[1],
        gains[1],
        True,
        (dscaled_1, *spread_rows(stats)),
    )
    result = after_last_call(hidden, meet(kept_1[5:9]))
    grad_1 = back_last_call(hidden, meet(back_1[5:9]), gains[1], cot, mixed_0, factor_0)
    back_0 = backward_call(
        where,
        kept_0[:5],
        own_w[0],
        other_w[0],
        taps[0],
        taps_state[0],
        heads[0],
        gains[0],
        False,
        spread_rows(grad_1),
    )
    grad_0 = back_first_call(rows_in, meet(back_0[5:9]), gains[0], grad_1)

    def weight_grads(normed, rows_grad, back):
        d_own, d_other, dss, scaled_own, scaled_other = back[:5]
        grad_taps, grad_taps_state, grad_heads, grad_gain = back[9:13]
        theirs = jnp.concatenate(
            [dot_tn(normed, d_other).astype(BF), dot_tn(rows_grad, scaled_other).astype(BF)],
            axis=1,
        )
        given = swap(theirs).astype(F32)
        mine_in = dot_tn(normed, d_own) + given[:, :CHANNELS]
        mine_out = dot_tn(rows_grad, scaled_own) + given[:, CHANNELS:]
        shared = dot_tn(normed, dss)
        lines = jnp.concatenate([grad_taps[:6]], axis=0)
        lines = lines.reshape(6, 4, 2, 96).transpose(1, 3, 2, 0).reshape(384, 12)
        lines = lax.dynamic_update_slice_in_dim(
            jnp.zeros((D, 12), F32), lines, place * 384, 0
        )
        state_lines = jnp.pad(
            grad_taps_state[:5].T.reshape(16, 16, 5), ((0, 0), (0, 80), (0, 0))
        ).reshape(D, 5)
        head_lines = jnp.pad(grad_heads[:3, :HEADS].T, ((0, 84), (0, 0)))
        head_lines = jnp.tile(head_lines, (16, 1))
        payload = jnp.concatenate(
            [
                mine_in,
                mine_out,
                shared[:, : 256 + HEADS],
                lines,
                grad_gain.reshape(D, 1),
                state_lines,
                head_lines,
                jnp.zeros((D, 128 - 33), F32),
            ],
            axis=1,
        ).astype(BF)
        return lax.psum_scatter(payload, DP, scatter_dimension=0, tiled=True).astype(F32)

    share_1 = weight_grads(kept_1[0], cot_rows, back_1)
    share_0 = weight_grads(kept_0[0], back_0[13], back_0)
    share_own = jnp.where(is_first, share_0, share_1)
    share_got = swap(jnp.where(is_first, share_1, share_0).astype(BF)).astype(F32)
    halves_in = jnp.stack([share_own[:, :CHANNELS], share_got[:, :CHANNELS]], axis=1)
    grad_inner = jnp.where(is_first, halves_in, halves_in[:, ::-1])
    out_own = share_own[:, CHANNELS : CHANNELS + HALF]
    out_got = share_got[:, CHANNELS : CHANNELS + HALF]
    grad_output = jnp.where(
        is_first,
        jnp.concatenate([out_own, out_got], axis=1),
        jnp.concatenate([out_got, out_own], axis=1),
    ).T
    summed = (share_own + share_got)[:, CHANNELS + HALF :]
    misc = summed[:, 256:]
    grad_step = misc[:, :HEADS]
    grad_heads = misc[:HEADS, 30:33].T
    to_send = jnp.concatenate(
        [
            summed[:, :256].reshape(4, 6144),
            misc[:, 24].reshape(4, 24),
            misc[:, 12:24].reshape(96, 2, 6).transpose(1, 0, 2).reshape(4, 48 * 6),
            misc[:16, 25:30].reshape(4, 20),
            jnp.zeros((4, 32 * 256 - 6144 - 332), F32),
        ],
        axis=1,
    ).reshape(4, 32, 256)
    pieces = [pick(to_send, lax.rem(place + o, 4), 0) for o in range(4)]
    met = meet(pieces)
    total = (met[0] + met[1] + met[2] + met[3]).reshape(-1)
    grad_state = total[:6144].reshape(24, 256)
    grad_norm = total[6144:6168]
    inner_lines = total[6168:6456].reshape(48, 6).T
    grad_conv_inner = inner_lines[:5]
    grad_gate = inner_lines[5]
    grad_conv_state = total[6456:6476].reshape(4, 5).T
    rows_got = swap(jnp.where(is_first, result, grad_0))
    section_rows = jnp.where(
        is_first, jnp.stack([grad_0, rows_got]), jnp.stack([rows_got, result])
    )
    return (
        section_rows[None],
        grad_norm[None],
        grad_inner[None],
        grad_step[None],
        grad_state[None],
        grad_conv_inner[None],
        grad_conv_state[None],
        grad_gate[None],
        grad_heads[None],
        grad_output[None],
    )


def solution(mesh):
    split = Mesh(
        mesh.devices.reshape(mesh.shape["section"], 4, 4, mesh.shape["tensor"]),
        ("section", "dp_0", "dp_1", "tensor"),
    )
    return jax.shard_map(
        shards,
        mesh=split,
        in_specs=(
            P("section", None, DP_TENSOR, None),
            P("section", DP_TENSOR),
            P("section", DP, None, "tensor"),
            P("section", DP, "tensor"),
            P("section", DP_TENSOR, None),
            P("section", None, DP_TENSOR),
            P("section", None, DP_TENSOR),
            P("section", DP_TENSOR),
            P("section", None, "tensor"),
            P("section", "tensor", DP),
        ),
        out_specs=(
            P("section", None, DP_TENSOR, None),
            P("section", DP_TENSOR),
            P("section", DP, None, "tensor"),
            P("section", DP, "tensor"),
            P("section", DP_TENSOR, None),
            P("section", None, DP_TENSOR),
            P("section", None, DP_TENSOR),
            P("section", DP_TENSOR),
            P("section", None, "tensor"),
            P("section", "tensor", DP),
        ),
        check_vma=False,
    )
```

time: 2190 us -> 563 us (0.26)
  blocking collectives: 1170 us -> 13.1 us
  matrix products: 297 us -> 17 us
  local copies, waits for them, and re-layouts: 275 us -> 90.7 us
  other arithmetic: 189 us -> 21.6 us
  Pallas kernels: 0 us -> 109 us
  waiting for transfers between devices: 177 us -> 251 us
    unnamed x2 -> x0, blocking collectives: 525 us -> none
    all_gather x3 -> x1, blocking collectives: 537 us -> 13.1 us  [shards(): filled = lax.all_gather(packed, 'tensor', axis=0).reshape(4, 32 * 256)]
    dot_general x75 -> x10, matrix products: 286 us -> 17 us  [dot_tn(): lax.dot_general(left, right, (((0,), (0,)), ((), ())), preferred_element_...]
    ppermute x4 -> x39, waiting for transfers between devices: 3.63 us -> 113 us  [the longest x30 112 us: turn(): return lax.ppermute(v, 'tensor', [(i, (i + by) % 4) for i in range(4)])]
    pallas_call x0 -> x9, Pallas kernels: none -> 109 us  [the longest x2 58.5 us: backward_call(): pl.pallas_call(kernel, out_shape=out_shape, in_specs=[SMEM] + [VMEM] * (l...]
    all_gather x1 -> x2, waiting for transfers between devices: 0.01 us -> 104 us  [shards(): full = lax.all_gather(shard, DP, axis=0, tiled=True)]
    all_to_all x3 -> x0, blocking collectives: 87.5 us -> none  [the longest x2 63.5 us: summed_on_arrival(): parts = lax.all_to_all(split_up(x, dim, size), axis, 0, 0, tiled=True)]
    all_to_all x12 -> x0, waiting for transfers between devices: 77.9 us -> none  [the longest x11 77.9 us: copy_for_each(): return lax.all_to_all(copies, axis, split_axis=0, concat_axis=0, tiled=True)]
  transfers between devices with their start and end apart: 24 -> 43, of which waited for: 12 -> 19; matrix products, arithmetic and copies ran while one was open for 9% -> 15% of each run, Pallas kernels for 0% -> 11%
where the time goes in v1:
time: 563 us; the launch traced here: 556 us
  waiting for transfers between devices  251 us (45%)
  Pallas kernels  109 us (19%)
  local copies, waits for them, and re-layouts  90.7 us (16%)
  starting transfers between devices  38.6 us (7%)
  other arithmetic  21.6 us (4%)
  matrix products  17 us (3%)
  between operations  15.3 us (3%)
  blocking collectives  13.1 us (2%)
    ppermute x30, waiting for transfers between devices, turn(): return lax.ppermute(v, 'tensor', [(i, (i + by) % 4) for i in range(4)])  112 us
    all_gather x2, waiting for transfers between devices, shards(): full = lax.all_gather(shard, DP, axis=0, tiled=True)  104 us
    pallas_call x2, Pallas kernels, backward_call(): pl.pallas_call(kernel, out_shape=out_shape, in_specs=[SMEM] + [VMEM] * (l...  58.5 us
    ppermute x30, starting transfers between devices, turn(): return lax.ppermute(v, 'tensor', [(i, (i + by) % 4) for i in range(4)])  36.4 us
    pallas_call x2, Pallas kernels, forward_call(): pl.pallas_call(kernel, out_shape=out_shape, in_specs=[SMEM] + [VMEM] * (l...  36.4 us
    reduce_scatter x2, waiting for transfers between devices, weight_grads(): lax.psum_scatter(payload, DP, scatter_dimension=0, tiled=True).astype(F32)  32.1 us
    concatenate x2, local copies, waits for them, and re-layouts, weight_grads(): jnp.concatenate([mine_in, mine_out, shared[:, :256 + HEADS], lines, grad_...  17.5 us
    dot_general x10, matrix products, dot_tn(): lax.dot_general(left, right, (((0,), (0,)), ((), ())), preferred_element_...  17 us
  transfers between devices with their start and end apart: 43, of which 19 were waited for; matrix products, arithmetic and copies ran while one was open for 15% of the time, Pallas kernels for 11%

profile of v1, /device:TPU:0, one launch (start us, length us, event | category | flops | bytes accessed | tf_op | source)
XLA Modules:
  0.0 556.0 jit_solution(4183322185397972182)
XLA Ops:
  11.0 13.1 %all_gather.9 = bf16[4,32,256]{2,1,0:T(8,128)(2,1)S(1)} all-gather(bf16[1,32,256]{2,1,0:T(8,128)(2,1)S(1)} %all_gather_reshape.3), channel_id=1, replica_groups=mesh['section'=2,'dp_0'=4,'dp_1'=4,'tensor'=4] {'tensor'}, dimensions={0}, use_global_device_ids=true | all-gather | bytes 81920 | tf_op jit(solution)/shard_map/all_gather | solution.py:649
  31.9 54.5 %all-gather.3.cloned.1.call-done.refs_5_.refs_6_ = bf16[1536,1536]{1,0:T(8,128)(2,1)} async-done(((bf16[96,1536]{1,0:T(8,128)(2,1)}), bf16[1536,1536]{1,0:T(8,128)(2,1)}) %all-gather.3.cloned.1.call-update) | async-done | bytes 4718608 | tf_op jit(solution)/shard_map/all_gather | solution.py:668
  86.4 4.1 slice.211
  92.8 49.9 %all-gather.5.cloned.1.call-done.refs_5_.refs_6_ = bf16[1536,1536]{1,0:T(8,128)(2,1)} async-done(((bf16[96,1536]{1,0:T(8,128)(2,1)}), bf16[1536,1536]{1,0:T(8,128)(2,1)}) %all-gather.5.cloned.1.call-update) | async-done | bytes 4718608 | tf_op jit(solution)/shard_map/all_gather | solution.py:668
  142.7 4.1 slice.215
  184.8 16.7 %layer_forward.2 = (bf16[512,1536]{1,0:T(8,128)(2,1)}, f32[2,512,768]{2,1,0:T(8,128)}, f32[512,384]{1,0:T(8,128)}, f32[512,768]{1,0:T(8,128)}, bf16[4,128,768]{2...) custom-call(s32[2]{0:T(128)} %pad_add_fusion.refs_0_, ...), custom_call_target="tpu_custom_call" | custom-call | tf_op jit(solution)/shard_map/layer_forward/pallas_call | solution.py:251
  205.6 19.2 %collective-permute-done.7.b = bf16[128,1664]{1,0:T(8,128)(2,1)S(1)} collective-permute-done((bf16[128,1664]{1,0:T(8,128)(2,1)}, bf16[128,1664]{1,0:T(8,128)(2,1)S(1)}, u32[]{:S(2)}, u32[]{:S(2)}) %collective-permute-start.7) | collective-permute-done | bytes 426016 | tf_op jit(solution)/shard_map/ppermute | solution.py:599
  226.8 3.1 between_layers.1
  232.1 9.5 %collective-permute-done.14.refs_11_ = bf16[128,1536]{1,0:T(8,128)(2,1)S(1)} collective-permute-done((bf16[128,1536]{1,0:T(8,128)(2,1)}, bf16[128,1536]{1,0:T(8,128)(2,1)S(1)}, u32[]{:S(2)}, u32[]{:S(2)}) %collective-permute-start.14) | collective-permute-done | bytes 393248 | tf_op jit(solution)/shard_map/ppermute | solution.py:599
  244.3 12.9 %collective-permute-done.10.refs_2_ = bf16[128,1536]{1,0:T(8,128)(2,1)S(1)} collective-permute-done((bf16[128,1536]{1,0:T(8,128)(2,1)}, bf16[128,1536]{1,0:T(8,128)(2,1)S(1)}, u32[]{:S(2)}, u32[]{:S(2)}) %collective-permute-start.10) | collective-permute-done | bytes 393248 | tf_op jit(solution)/shard_map/ppermute | solution.py:599
  258.1 19.7 %layer_forward.3 = (bf16[512,1536]{1,0:T(8,128)(2,1)}, f32[2,512,768]{2,1,0:T(8,128)}, f32[512,384]{1,0:T(8,128)}, f32[512,768]{1,0:T(8,128)}, bf16[4,128,768]{2...) custom-call(s32[2]{0:T(128)} %pad_add_fusion.refs_0_, ...), custom_call_target="tpu_custom_call" | custom-call | tf_op jit(solution)/shard_map/layer_forward/pallas_call | solution.py:251
  283.2 3.4 collective-permute-done.19.refs_16_
  287.2 28.3 %layer_backward.2 = (bf16[512,768]{1,0:T(8,128)(2,1)}, bf16[512,768]{1,0:T(8,128)(2,1)}, bf16[512,384]{1,0:T(8,128)(2,1)}, bf16[512,384]{1,0:T(8,128)(2,1)}, bf1...) custom-call(s32[2]{0:T(128)} %pad_add_fusion.refs_0_, ...), custom_call_target="tpu_custom_call" | custom-call | tf_op jit(solution)/shard_map/layer_backward/pallas_call | solution.py:472
  315.6 2.7 convolution_convert_fusion
  328.8 2.6 convert_element_type.68
  335.7 8.7 %concatenate.74 = bf16[1536,1536]{1,0:T(8,128)(2,1)} concatenate(bf16[1536,768]{1,0:T(8,128)(2,1)S(1)} %fusion, bf16[1536,384]{1,0:T(8,128)(2,1)S(1)} %fusion.3, bf16[1536,268]{1,0:T(8,128)(2,1)} %bitcast.167, bf16[1536,12]{1,0:T(8,128)(2,1)} %constant_dynamic-update-slice_fusion, bf16[1536,1]{1,0:T(8,128)(2,1)} %copy.140, bf16[1536,5]{1,0:T(8,128)(2,1)} %bitcast.166, ...), dimensions={1} | concatenate | bytes 9437184 | tf_op jit(solution)/shard_map/concatenate | solution.py:755
  345.5 3.1 collective-permute-start.21
  348.7 17.9 %collective-permute-done.20.b = bf16[128,1536]{1,0:T(8,128)(2,1)S(1)} collective-permute-done((bf16[128,1536]{1,0:T(8,128)(2,1)S(1)}, bf16[128,1536]{1,0:T(8,128)(2,1)S(1)}, u32[]{:S(2)}, u32[]{:S(2)}) %collective-permute-start.20) | collective-permute-done | bytes 393248 | tf_op jit(solution)/shard_map/ppermute | solution.py:599
  367.7 3.3 between_layers_back.1.refs_12_.grad_ref
  375.2 8.7 %collective-permute-done.23.refs_13_ = bf16[128,1664]{1,0:T(8,128)(2,1)S(1)} collective-permute-done((bf16[128,1664]{1,0:T(8,128)(2,1)}, bf16[128,1664]{1,0:T(8,128)(2,1)S(1)}, u32[]{:S(2)}, u32[]{:S(2)}) %collective-permute-start.23) | collective-permute-done | bytes 426016 | tf_op jit(solution)/shard_map/ppermute | solution.py:599
  383.9 8.1 %collective-permute-done.24.refs_14_ = bf16[128,1664]{1,0:T(8,128)(2,1)S(1)} collective-permute-done((bf16[128,1664]{1,0:T(8,128)(2,1)}, bf16[128,1664]{1,0:T(8,128)(2,1)S(1)}, u32[]{:S(2)}, u32[]{:S(2)}) %collective-permute-start.24) | collective-permute-done | bytes 426016 | tf_op jit(solution)/shard_map/ppermute | solution.py:599
  394.5 30.2 %layer_backward.3 = (bf16[512,768]{1,0:T(8,128)(2,1)}, bf16[512,768]{1,0:T(8,128)(2,1)}, bf16[512,384]{1,0:T(8,128)(2,1)}, bf16[512,384]{1,0:T(8,128)(2,1)}, bf1...) custom-call(s32[2]{0:T(128)} %pad_add_fusion.refs_0_, ...), custom_call_target="tpu_custom_call" | custom-call | tf_op jit(solution)/shard_map/layer_backward/pallas_call | solution.py:472
  424.7 2.6 convolution_convert_fusion.3
  445.0 8.7 %concatenate.72 = bf16[1536,1536]{1,0:T(8,128)(2,1)} concatenate(bf16[1536,768]{1,0:T(8,128)(2,1)S(1)} %fusion.1, bf16[1536,384]{1,0:T(8,128)(2,1)S(1)} %fusion.2, bf16[1536,268]{1,0:T(8,128)(2,1)} %bitcast.168, bf16[1536,12]{1,0:T(8,128)(2,1)} %constant_dynamic-update-slice_fusion.1, bf16[1536,1]{1,0:T(8,128)(2,1)} %copy.130, bf16[1536,5]{1,0:T(8,128)(2,1)} %bitcast.165, ...), dimensions={1} | concatenate | bytes 9437184 | tf_op jit(solution)/shard_map/concatenate | solution.py:755
  461.2 15.5 %collective-permute-done.29.b = bf16[128,1664]{1,0:T(8,128)(2,1)S(1)} collective-permute-done((bf16[128,1664]{1,0:T(8,128)(2,1)}, bf16[128,1664]{1,0:T(8,128)(2,1)S(1)}, u32[]{:S(2)}, u32[]{:S(2)}) %collective-permute-start.29) | collective-permute-done | bytes 426016 | tf_op jit(solution)/shard_map/ppermute | solution.py:599
  478.0 2.7 last_rows.1
  480.8 4.4 collective-permute-done.26.b
  485.2 7.4 %collective-permute-done.27.c = bf16[128,1536]{1,0:T(8,128)(2,1)S(1)} collective-permute-done((bf16[128,1536]{1,0:T(8,128)(2,1)}, bf16[128,1536]{1,0:T(8,128)(2,1)S(1)}, u32[]{:S(2)}, u32[]{:S(2)}) %collective-permute-start.27) | collective-permute-done | bytes 393248 | tf_op jit(solution)/shard_map/ppermute | solution.py:599
  494.5 3.1 first_rows_back.1
  498.7 32.1 %reduce-scatter.3.cloned.1.call-done = bf16[96,1536]{1,0:T(8,128)(2,1)} async-done(((bf16[1536,1536]{1,0:T(8,128)(2,1)}), bf16[96,1536]{1,0:T(8,128)(2,1)}) %reduce-scatter.3.cloned.1.call-update) | async-done | bytes 294928 | tf_op jit(solution)/shard_map/reduce_scatter | solution.py:768
  532.1 2.7 maximum_select_fusion
  536.2 3.3 collective-permute-start.38
  (365 shorter events, 134.2 us)
Async XLA Ops:
  7.2 79.2 %all-gather.3.cloned.1.call-start = ((), (), s32[]{:S(2)}) async-start(), calls=%async_computation.2 | async-start | bytes 5013504 | tf_op jit(solution)/shard_map/all_gather | solution.py:668
  31.1 111.6 %all-gather.5.cloned.1.call-start = ((), (), s32[]{:S(2)}) async-start(), calls=%async_computation.3 | async-start | bytes 5013504 | tf_op jit(solution)/shard_map/all_gather | solution.py:668
  31.9 466.8 %reduce-scatter.5.cloned.1.call-start = ((), (), s32[]{:S(2)}) async-start(), calls=%async_computation.5 | async-start | bytes 5013504 | tf_op jit(solution)/shard_map/reduce_scatter | solution.py:768
  90.5 92.4 %collective-permute-start.5 = (bf16[1536,1152]{1,0:T(8,128)(2,1)}, bf16[1536,1152]{1,0:T(8,128)(2,1)S(1)}, u32[]{:S(2)}, u32[]{:S(2)}) collective-permute-start(bf16[1536,1152]{1,0:T(8,128)(2,1)} %slice.211), channel_id=1, source_target_pairs={{0,64},{64,0},{1,65},{65,1},{2,66},{66,2},{3,67},{67,3},{4,68},{68... | collective-permute-start | bytes 10616840 | tf_op jit(solution)/shard_map/ppermute | solution.py:595
  92.2 57.9 %collective-permute-start = (bf16[128,1536]{1,0:T(8,128)(2,1)}, bf16[128,1536]{1,0:T(8,128)(2,1)}, u32[]{:S(2)}, u32[]{:S(2)}) collective-permute-start(bf16[128,1536]{1,0:T(8,128)(2,1)} %dynamic-slice_bitcast_fusion), channel_id=1, source_target_pairs={{0,64},{64,0},{1,65},{65,1},{2,66},{66,2},{3,67},{67,3},{4,68},{68... | collective-permute-start | bytes 1179656 | tf_op jit(solution)/shard_map/ppermute | solution.py:595
  92.8 55.2 %collective-permute-start.6 = (bf16[3,12]{1,0:T(4,128)(2,1)S(1)}, bf16[3,12]{1,0:T(4,128)(2,1)S(1)}, u32[]{:S(2)}, u32[]{:S(2)}) collective-permute-start(bf16[3,12]{1,0:T(4,128)(2,1)S(1)} %bitcast.208), channel_id=1, source_target_pairs={{0,64},{64,0},{1,65},{65,1},{2,66},{66,2},{3,67},{67,3},{4,68},{68... | collective-permute-start | bytes 224 | tf_op jit(solution)/shard_map/ppermute | solution.py:595
  146.8 97.5 %collective-permute-start.13 = (bf16[1536,1152]{1,0:T(8,128)(2,1)}, bf16[1536,1152]{1,0:T(8,128)(2,1)}, u32[]{:S(2)}, u32[]{:S(2)}) collective-permute-start(bf16[1536,1152]{1,0:T(8,128)(2,1)} %slice.215), channel_id=1, source_target_pairs={{0,64},{64,0},{1,65},{65,1},{2,66},{66,2},{3,67},{67,3},{4,68},{68... | collective-permute-start | bytes 10616840 | tf_op jit(solution)/shard_map/ppermute | solution.py:595
  157.3 25.6 %collective-permute-start.2 = (bf16[128,1536]{1,0:T(8,128)(2,1)}, bf16[128,1536]{1,0:T(8,128)(2,1)}, u32[]{:S(2)}, u32[]{:S(2)}) collective-permute-start(bf16[128,1536]{1,0:T(8,128)(2,1)} %norm_rows.1.refs_1_), channel_id=1, source_target_pairs={{0,1},{1,2},{2,3},{3,0},{4,5},{5,6},{6,7},{7,4},{8,9},{9,10},{10,1... | collective-permute-start | bytes 1179656 | tf_op jit(solution)/shard_map/ppermute | solution.py:599
  158.9 24.0 %collective-permute-start.3 = (bf16[128,1536]{1,0:T(8,128)(2,1)}, bf16[128,1536]{1,0:T(8,128)(2,1)}, u32[]{:S(2)}, u32[]{:S(2)}) collective-permute-start(bf16[128,1536]{1,0:T(8,128)(2,1)} %norm_rows.1.refs_1_), channel_id=1, source_target_pairs={{0,3},{1,0},{2,1},{3,2},{4,7},{5,4},{6,5},{7,6},{8,11},{9,8},{10,9... | collective-permute-start | bytes 1179656 | tf_op jit(solution)/shard_map/ppermute | solution.py:599
  160.6 22.4 %collective-permute-start.4 = (bf16[128,1536]{1,0:T(8,128)(2,1)}, bf16[128,1536]{1,0:T(8,128)(2,1)}, u32[]{:S(2)}, u32[]{:S(2)}) collective-permute-start(bf16[128,1536]{1,0:T(8,128)(2,1)} %norm_rows.1.refs_1_), channel_id=1, source_target_pairs={{0,2},{1,3},{2,0},{3,1},{4,6},{5,7},{6,4},{7,5},{8,10},{9,11},{10,... | collective-permute-start | bytes 1179656 | tf_op jit(solution)/shard_map/ppermute | solution.py:599
  201.4 23.3 %collective-permute-start.7 = (bf16[128,1664]{1,0:T(8,128)(2,1)}, bf16[128,1664]{1,0:T(8,128)(2,1)S(1)}, u32[]{:S(2)}, u32[]{:S(2)}) collective-permute-start(bf16[128,1664]{1,0:T(8,128)(2,1)} %get-tuple-element.68), channel_id=1, source_target_pairs={{0,1},{1,2},{2,3},{3,0},{4,5},{5,6},{6,7},{7,4},{8,9},{9,10},{10,1... | collective-permute-start | bytes 1277960 | tf_op jit(solution)/shard_map/ppermute | solution.py:599
  202.1 23.8 %collective-permute-start.8 = (bf16[128,1664]{1,0:T(8,128)(2,1)}, bf16[128,1664]{1,0:T(8,128)(2,1)S(1)}, u32[]{:S(2)}, u32[]{:S(2)}) collective-permute-start(bf16[128,1664]{1,0:T(8,128)(2,1)} %get-tuple-element.69), channel_id=1, source_target_pairs={{0,3},{1,0},{2,1},{3,2},{4,7},{5,4},{6,5},{7,6},{8,11},{9,8},{10,9... | collective-permute-start | bytes 1277960 | tf_op jit(solution)/shard_map/ppermute | solution.py:599
  204.7 21.2 %collective-permute-start.9 = (bf16[128,1664]{1,0:T(8,128)(2,1)}, bf16[128,1664]{1,0:T(8,128)(2,1)S(1)}, u32[]{:S(2)}, u32[]{:S(2)}) collective-permute-start(bf16[128,1664]{1,0:T(8,128)(2,1)} %get-tuple-element.70), channel_id=1, source_target_pairs={{0,2},{1,3},{2,0},{3,1},{4,6},{5,7},{6,4},{7,5},{8,10},{9,11},{10,... | collective-permute-start | bytes 1277960 | tf_op jit(solution)/shard_map/ppermute | solution.py:599
  205.1 36.5 %collective-permute-start.14 = (bf16[128,1536]{1,0:T(8,128)(2,1)}, bf16[128,1536]{1,0:T(8,128)(2,1)S(1)}, u32[]{:S(2)}, u32[]{:S(2)}) collective-permute-start(bf16[128,1536]{1,0:T(8,128)(2,1)} %get-tuple-element.146.refs_10_.grad_ref), channel_id=1, source_target_pairs={{0,1},{1,2},{2,3},{3,0},{4,5},{5,6},{6,7},{7,4},{8,9},{9,10},{10,1... | collective-permute-start | bytes 1179656 | tf_op jit(solution)/shard_map/ppermute | solution.py:599
  224.8 16.9 %collective-permute-start.15 = (bf16[128,1536]{1,0:T(8,128)(2,1)}, bf16[128,1536]{1,0:T(8,128)(2,1)S(1)}, u32[]{:S(2)}, u32[]{:S(2)}) collective-permute-start(bf16[128,1536]{1,0:T(8,128)(2,1)} %get-tuple-element.146.refs_10_.grad_ref), channel_id=1, source_target_pairs={{0,3},{1,0},{2,1},{3,2},{4,7},{5,4},{6,5},{7,6},{8,11},{9,8},{10,9... | collective-permute-start | bytes 1179656 | tf_op jit(solution)/shard_map/ppermute | solution.py:599
  225.9 18.4 %collective-permute-start.16 = (bf16[128,1536]{1,0:T(8,128)(2,1)}, bf16[128,1536]{1,0:T(8,128)(2,1)S(1)}, u32[]{:S(2)}, u32[]{:S(2)}) collective-permute-start(bf16[128,1536]{1,0:T(8,128)(2,1)} %get-tuple-element.146.refs_10_.grad_ref), channel_id=1, source_target_pairs={{0,2},{1,3},{2,0},{3,1},{4,6},{5,7},{6,4},{7,5},{8,10},{9,11},{10,... | collective-permute-start | bytes 1179656 | tf_op jit(solution)/shard_map/ppermute | solution.py:599
  229.9 27.2 %collective-permute-start.10 = (bf16[128,1536]{1,0:T(8,128)(2,1)}, bf16[128,1536]{1,0:T(8,128)(2,1)S(1)}, u32[]{:S(2)}, u32[]{:S(2)}) collective-permute-start(bf16[128,1536]{1,0:T(8,128)(2,1)} %get-tuple-element.72.refs_1_), channel_id=1, source_target_pairs={{0,1},{1,2},{2,3},{3,0},{4,5},{5,6},{6,7},{7,4},{8,9},{9,10},{10,1... | collective-permute-start | bytes 1179656 | tf_op jit(solution)/shard_map/ppermute | solution.py:599
  241.6 15.5 %collective-permute-start.11 = (bf16[128,1536]{1,0:T(8,128)(2,1)}, bf16[128,1536]{1,0:T(8,128)(2,1)S(1)}, u32[]{:S(2)}, u32[]{:S(2)}) collective-permute-start(bf16[128,1536]{1,0:T(8,128)(2,1)} %get-tuple-element.72.refs_1_), channel_id=1, source_target_pairs={{0,3},{1,0},{2,1},{3,2},{4,7},{5,4},{6,5},{7,6},{8,11},{9,8},{10,9... | collective-permute-start | bytes 1179656 | tf_op jit(solution)/shard_map/ppermute | solution.py:599
  241.6 15.5 %collective-permute-start.12 = (bf16[128,1536]{1,0:T(8,128)(2,1)}, bf16[128,1536]{1,0:T(8,128)(2,1)S(1)}, u32[]{:S(2)}, u32[]{:S(2)}) collective-permute-start(bf16[128,1536]{1,0:T(8,128)(2,1)} %get-tuple-element.72.refs_1_), channel_id=1, source_target_pairs={{0,2},{1,3},{2,0},{3,1},{4,6},{5,7},{6,4},{7,5},{8,10},{9,11},{10,... | collective-permute-start | bytes 1179656 | tf_op jit(solution)/shard_map/ppermute | solution.py:599
  344.5 186.3 %reduce-scatter.3.cloned.1.call-start = ((), (), s32[]{:S(2)}) async-start(), calls=%async_computation.4 | async-start | bytes 5013504 | tf_op jit(solution)/shard_map/reduce_scatter | solution.py:768
  345.4 21.1 %collective-permute-start.20 = (bf16[128,1536]{1,0:T(8,128)(2,1)S(1)}, bf16[128,1536]{1,0:T(8,128)(2,1)S(1)}, u32[]{:S(2)}, u32[]{:S(2)}) collective-permute-start(bf16[128,1536]{1,0:T(8,128)(2,1)S(1)} %copy-done.61), channel_id=1, source_target_pairs={{0,1},{1,2},{2,3},{3,0},{4,5},{5,6},{6,7},{7,4},{8,9},{9,10},{10,1... | collective-permute-start | bytes 1179656 | tf_op jit(solution)/shard_map/ppermute | solution.py:599
  345.5 21.0 %collective-permute-start.21 = (bf16[128,1536]{1,0:T(8,128)(2,1)S(1)}, bf16[128,1536]{1,0:T(8,128)(2,1)S(1)}, u32[]{:S(2)}, u32[]{:S(2)}) collective-permute-start(bf16[128,1536]{1,0:T(8,128)(2,1)S(1)} %copy-done.60), channel_id=1, source_target_pairs={{0,3},{1,0},{2,1},{3,2},{4,7},{5,4},{6,5},{7,6},{8,11},{9,8},{10,9... | collective-permute-start | bytes 1179656 | tf_op jit(solution)/shard_map/ppermute | solution.py:599
  348.7 17.9 %collective-permute-start.22 = (bf16[128,1536]{1,0:T(8,128)(2,1)S(1)}, bf16[128,1536]{1,0:T(8,128)(2,1)S(1)}, u32[]{:S(2)}, u32[]{:S(2)}) collective-permute-start(bf16[128,1536]{1,0:T(8,128)(2,1)S(1)} %copy-done.59), channel_id=1, source_target_pairs={{0,2},{1,3},{2,0},{3,1},{4,6},{5,7},{6,4},{7,5},{8,10},{9,11},{10,... | collective-permute-start | bytes 1179656 | tf_op jit(solution)/shard_map/ppermute | solution.py:599
  371.6 20.3 %collective-permute-start.24 = (bf16[128,1664]{1,0:T(8,128)(2,1)}, bf16[128,1664]{1,0:T(8,128)(2,1)S(1)}, u32[]{:S(2)}, u32[]{:S(2)}) collective-permute-start(bf16[128,1664]{1,0:T(8,128)(2,1)} %between_layers_back.1.refs_12_.grad_ref), channel_id=1, source_target_pairs={{0,3},{1,0},{2,1},{3,2},{4,7},{5,4},{6,5},{7,6},{8,11},{9,8},{10,9... | collective-permute-start | bytes 1277960 | tf_op jit(solution)/shard_map/ppermute | solution.py:599
  374.2 19.5 %collective-permute-start.25 = (bf16[128,1664]{1,0:T(8,128)(2,1)}, bf16[128,1664]{1,0:T(8,128)(2,1)S(1)}, u32[]{:S(2)}, u32[]{:S(2)}) collective-permute-start(bf16[128,1664]{1,0:T(8,128)(2,1)} %between_layers_back.1.refs_12_.grad_ref), channel_id=1, source_target_pairs={{0,2},{1,3},{2,0},{3,1},{4,6},{5,7},{6,4},{7,5},{8,10},{9,11},{10,... | collective-permute-start | bytes 1277960 | tf_op jit(solution)/shard_map/ppermute | solution.py:599
  453.8 23.0 %collective-permute-start.29 = (bf16[128,1664]{1,0:T(8,128)(2,1)}, bf16[128,1664]{1,0:T(8,128)(2,1)S(1)}, u32[]{:S(2)}, u32[]{:S(2)}) collective-permute-start(bf16[128,1664]{1,0:T(8,128)(2,1)} %get-tuple-element.91), channel_id=1, source_target_pairs={{0,1},{1,2},{2,3},{3,0},{4,5},{5,6},{6,7},{7,4},{8,9},{9,10},{10,1... | collective-permute-start | bytes 1277960 | tf_op jit(solution)/shard_map/ppermute | solution.py:599
  455.0 21.8 %collective-permute-start.30 = (bf16[128,1664]{1,0:T(8,128)(2,1)S(1)}, bf16[128,1664]{1,0:T(8,128)(2,1)S(1)}, u32[]{:S(2)}, u32[]{:S(2)}) collective-permute-start(bf16[128,1664]{1,0:T(8,128)(2,1)S(1)} %copy-done.58), channel_id=1, source_target_pairs={{0,3},{1,0},{2,1},{3,2},{4,7},{5,4},{6,5},{7,6},{8,11},{9,8},{10,9... | collective-permute-start | bytes 1277960 | tf_op jit(solution)/shard_map/ppermute | solution.py:599
  457.1 20.2 %collective-permute-start.31 = (bf16[128,1664]{1,0:T(8,128)(2,1)S(1)}, bf16[128,1664]{1,0:T(8,128)(2,1)S(1)}, u32[]{:S(2)}, u32[]{:S(2)}) collective-permute-start(bf16[128,1664]{1,0:T(8,128)(2,1)S(1)} %copy-done.57), channel_id=1, source_target_pairs={{0,2},{1,3},{2,0},{3,1},{4,6},{5,7},{6,4},{7,5},{8,10},{9,11},{10,... | collective-permute-start | bytes 1277960 | tf_op jit(solution)/shard_map/ppermute | solution.py:599
  458.0 27.2 %collective-permute-start.26 = (bf16[128,1536]{1,0:T(8,128)(2,1)}, bf16[128,1536]{1,0:T(8,128)(2,1)S(1)}, u32[]{:S(2)}, u32[]{:S(2)}) collective-permute-start(bf16[128,1536]{1,0:T(8,128)(2,1)} %get-tuple-element.87), channel_id=1, source_target_pairs={{0,1},{1,2},{2,3},{3,0},{4,5},{5,6},{6,7},{7,4},{8,9},{9,10},{10,1... | collective-permute-start | bytes 1179656 | tf_op jit(solution)/shard_map/ppermute | solution.py:599
  458.7 33.9 %collective-permute-start.27 = (bf16[128,1536]{1,0:T(8,128)(2,1)}, bf16[128,1536]{1,0:T(8,128)(2,1)S(1)}, u32[]{:S(2)}, u32[]{:S(2)}) collective-permute-start(bf16[128,1536]{1,0:T(8,128)(2,1)} %get-tuple-element.88), channel_id=1, source_target_pairs={{0,3},{1,0},{2,1},{3,2},{4,7},{5,4},{6,5},{7,6},{8,11},{9,8},{10,9... | collective-permute-start | bytes 1179656 | tf_op jit(solution)/shard_map/ppermute | solution.py:599
  476.8 16.9 %collective-permute-start.28 = (bf16[128,1536]{1,0:T(8,128)(2,1)}, bf16[128,1536]{1,0:T(8,128)(2,1)S(1)}, u32[]{:S(2)}, u32[]{:S(2)}) collective-permute-start(bf16[128,1536]{1,0:T(8,128)(2,1)} %get-tuple-element.89), channel_id=1, source_target_pairs={{0,2},{1,3},{2,0},{3,1},{4,6},{5,7},{6,4},{7,5},{8,10},{9,11},{10,... | collective-permute-start | bytes 1179656 | tf_op jit(solution)/shard_map/ppermute | solution.py:599
  497.7 34.3 %collective-permute-start.32 = (f32[128,1536]{1,0:T(8,128)S(1)}, f32[128,1536]{1,0:T(8,128)}, u32[]{:S(2)}, u32[]{:S(2)}) collective-permute-start(f32[128,1536]{1,0:T(8,128)S(1)} %broadcast_select_fusion), channel_id=1, source_target_pairs={{0,64},{64,0},{1,65},{65,1},{2,66},{66,2},{3,67},{67,3},{4,68},{68... | collective-permute-start | bytes 2359304 | tf_op jit(solution)/shard_map/ppermute | solution.py:595
  (76 other events, 512.5 us)
Sparse Core Ops, SparseCore 0:
  31.2 55.0 all-gather.2
  89.1 53.5 all-gather.4
  344.6 76.8 reduce-scatter.4
  453.9 76.7 reduce-scatter.2
